TPU v7x, 128 devices: a whole 4x4x4 slice. The times are simulated.
128 devices in a mesh: samp: 8 (over z, core), term: 16 (over y, x).
Axes of the slice: x: 4, y: 4, z: 4, core: 2. Of those that a mesh axis runs over, the one named last changes fastest.
Arguments:
- basis: bfloat16 [8192, 4096], P('samp', 'term'), may hold values from -0.143631065 to 0.143631065
- strain: float32 [8192, 4096], P(('samp', 'term')), may hold values from -17 to 17
- route: int32 [8192], replicated, may hold values from 0 to 8191, as said below
- chosen: int32 [3], replicated, may hold values from 0 to 63, as said below
Outputs:
- residual: float32 [8192, 4096], P('samp', 'term')
- coefficients: float32 [192, 4096], P(None, 'term')
- scores: float32 [3, 64], P(None, 'term')
Inputs may be any that keep to these rules, and one draw needn't show every extreme that they name: route is a permutation of the sample indices; of each aligned block of 64 evolutions exactly 8 go to each aligned block of 1024 samples. `chosen`: the 3 selected blocks are distinct.
All inputs are finite; a program needn't handle non-finite values.
Results may differ from a plain program's by a relative error of at most 0.003.
Values may be sent and summed in bfloat16 or wider, within the bound.
A program may use at most 128 MiB of HBM per device.

v0:
```python
import jax
import jax.numpy as jnp
from jax import lax
from jax.sharding import PartitionSpec as P

BLOCK = 64
STEPS = 3


highest = lax.Precision.HIGHEST
epsilon = 1e-06


def from_root(shard, axis, root):
    mine = lax.axis_index(axis) == root
    return lax.psum(jnp.where(mine, shard, jnp.zeros_like(shard)), axis)


def contract(first_arg, second_arg):
    return lax.dot_general(
        first_arg,
        second_arg,
        (((0,), (0,)), ((), ())),
        precision=highest,
        preferred_element_type=jnp.float32,
    )


def product(first_arg, second_arg):
    return jnp.dot(first_arg, second_arg, precision=highest, preferred_element_type=jnp.float32)


def make_term(basis, rounded):
    return lax.dot_general(
        rounded, basis, (((0,), (0,)), ((), ())), preferred_element_type=jnp.float32
    )


def score_row(scattered, block_count, regions):
    squares = (scattered * scattered).reshape(scattered.shape[0], block_count, BLOCK)
    totals = lax.psum(jnp.sum(squares, axis=(0, 2)), "samp")
    return jnp.sqrt(totals / (BLOCK * regions) + epsilon)


def local(basis, strain, route, chosen):
    samp_n = lax.axis_size("samp")
    term_n = lax.axis_size("term")
    sim_rows, regions = strain.shape
    samp_rows = sim_rows * term_n
    total_rows = samp_rows * samp_n
    capacity = sim_rows // samp_n
    block_count = basis.shape[1] // BLOCK
    region_slab = regions // term_n
    samp_index = lax.axis_index("samp")
    term_index = lax.axis_index("term")
    device_index = samp_index * term_n + term_index
    own_route = lax.dynamic_slice_in_dim(route, device_index * sim_rows, sim_rows)
    send_order = jnp.argsort(own_route // samp_rows, stable=True)
    outgoing = strain[send_order].reshape(samp_n, capacity, regions)
    arrived = lax.all_to_all(outgoing, "samp", split_axis=0, concat_axis=0, tiled=True).reshape(
        sim_rows, regions
    )
    gathered = lax.all_gather(arrived, "term", axis=0, tiled=True)
    route_grid = route.reshape(samp_n, term_n, sim_rows)
    is_target = route_grid // samp_rows == samp_index
    rank_within = jnp.cumsum(is_target.astype(jnp.int32), axis=2) - 1
    source_block = lax.broadcasted_iota(jnp.int32, route_grid.shape, 0)
    term_source = lax.broadcasted_iota(jnp.int32, route_grid.shape, 1)
    arrival = term_source * sim_rows + source_block * capacity + rank_within
    target_slot = jnp.where(is_target, route_grid % samp_rows, samp_rows)
    inverse = (
        jnp.zeros((samp_rows,), jnp.int32)
        .at[target_slot.reshape(-1)]
        .set(arrival.reshape(-1), mode="drop")
    )
    residual = gathered[inverse]
    basis_kept = None
    score_list = []
    coef_list = []
    for pursuit in range(STEPS):
        current = lax.psum_scatter(
            make_term(basis, residual.astype(jnp.bfloat16)).astype(jnp.bfloat16),
            "samp",
            scatter_dimension=0,
            tiled=True,
        ).astype(jnp.float32)
        score_list.append(score_row(current, block_count, regions))
        chosen_block = chosen[pursuit]
        owner_index = chosen_block // block_count
        local_start = chosen_block % block_count * BLOCK
        block_piece = lax.dynamic_slice_in_dim(basis, local_start, BLOCK, 1)
        picked = from_root(block_piece, "term", owner_index).astype(jnp.float32)
        if pursuit > 0:
            projection = (
                lax.psum(contract(basis_kept, picked).astype(jnp.bfloat16), "samp").astype(
                    jnp.float32
                )
                / total_rows
            )
            picked = picked - product(basis_kept, projection)
        gram_matrix, cross_terms = lax.psum(
            (contract(picked, picked), contract(picked, residual)), "samp"
        )
        lower_factor = jnp.linalg.cholesky(gram_matrix / total_rows)
        normed = lax.linalg.triangular_solve(
            lower_factor, picked, left_side=False, lower=True, transpose_a=True
        )
        coef_now = lax.linalg.triangular_solve(
            lower_factor, cross_terms / total_rows, left_side=True, lower=True
        )
        residual = residual - product(normed, coef_now)
        if basis_kept is None:
            basis_kept = normed
        else:
            basis_kept = jnp.concatenate([basis_kept, normed], axis=1)
        coef_list.append(
            lax.dynamic_slice_in_dim(coef_now, term_index * region_slab, region_slab, 1)
        )
    residual_slab = lax.dynamic_slice_in_dim(residual, term_index * region_slab, region_slab, 1)
    return (residual_slab, jnp.concatenate(coef_list, axis=0), jnp.stack(score_list, axis=0))


def solution(mesh):
    return jax.shard_map(
        local,
        mesh=mesh,
        in_specs=(P("samp", "term"), P(("samp", "term"), None), P(), P()),
        out_specs=(P("samp", "term"), P(None, "term"), P(None, "term")),
        check_vma=False,
    )
```

profile of v0, /device:TPU:1, one launch (start us, length us, event | category | flops | bytes accessed | tf_op | source)
XLA Modules:
  0.0 618.3 jit_solution(950504221052439087)
XLA Ops:
  12.0 6.8 %all-to-all-start = ((f32[8,8,4096]{2,1,0:T(8,128)}), f32[8,8,4096]{2,1,0:T(8,128)S(1)}, u32[]{:S(2)}, u32[]{:S(2)}) async-start(f32[8,8,4096]{2,1,0:T(8,128)} %bitcast), calls=%async_computation | async-start | bytes 2097152 | tf_op jit(solution)/shard_map/all_to_all | solution.py:60
  37.8 30.4 %scatter_custom_fusion = s32[1024]{0:T(1024)S(1)} fusion(s32[8192]{0:T(1024)S(1)} %compare_select_fusion, s32[8192]{0:T(1024)S(1)} %reshape.78, s32[]{:T(128)} %constant.153.clone.1), kind=kCustom, calls=%fused_computation.98 | custom fusion | bytes 4100 | tf_op jit(solution)/shard_map/scatter | solution.py:74
  68.3 48.0 %all-reduce.13.cloned.1.call-done = (bf16[1024,64]{0,1:T(8,128)(2,1)}, bf16[1024,64]{0,1:T(8,128)(2,1)}, bf16[1024,64]{0,1:T(8,128)(2,1)}) async-done(((bf16[1024,64]{0,1:T(8,128)(2,1)}, bf16[1024,64]{0,1:T(8,128)(2,1)}, bf16[1024,64]{0,1:T(8,128)(2,1)}), (bf16[1024,64]{0,1:T(8,128)(2,1)}, bf16[1024,64]{0,1:T(8,128)(2,1)}, bf16[1024,64]{0,1:T(8,128)(2,1)})) %all-reduce.13.cloned.1.call-update) | async-done | bytes 393232 | tf_op jit(solution)/shard_map/psum | solution.py:16
  117.4 23.3 %psum.99 = f32[64,64]{0,1:T(8,128)S(1)} all-reduce(f32[64,64]{0,1:T(8,128)S(1)} %fusion.62), channel_id=1, replica_groups=mesh['samp'=8,'term'=16] {'samp'}, use_global_device_ids=true, to_apply=%region_4.5 | all-reduce | flops 4096 | bytes 32768 | tf_op jit(solution)/shard_map/psum | solution.py:101
  140.8 5.8 cholesky.59
  148.0 4.9 custom-call.12
  152.9 78.1 %all-gather.2.cloned.1.call-done = f32[1024,4096]{1,0:T(8,128)} async-done(((f32[64,4096]{1,0:T(8,128)}), f32[1024,4096]{1,0:T(8,128)}) %all-gather.2.cloned.1.call-update) | async-done | bytes 16777232 | tf_op jit(solution)/shard_map/all_gather | solution.py:63
  231.0 20.4 %gather_fusion.1 = f32[1024,4096]{1,0:T(8,128)} fusion(f32[1024,4096]{1,0:T(8,128)} %all-gather.2.cloned.1.call-done, s32[1024]{0:T(1024)S(1)} %fusion.51), kind=kCustom, calls=%fused_computation.1 | custom fusion | bytes 33558528 | tf_op jit(solution)/shard_map/gather | solution.py:76
  251.5 11.2 %fusion.63 = f32[64,4096]{1,0:T(8,128)} fusion(bf16[1024,64]{0,1:T(8,128)(2,1)S(1)} %copy-done.6, f32[1024,4096]{1,0:T(8,128)} %gather_fusion.1), kind=kOutput, calls=%fused_computation.127 | convolution fusion | flops 3221225472 | bytes 17956864 | tf_op jit(solution)/shard_map/dot_general | solution.py:20
  263.4 23.3 %psum.102 = bf16[64,64]{0,1:T(8,128)(2,1)S(1)} all-reduce(bf16[64,64]{0,1:T(8,128)(2,1)S(1)} %convolution_convert_fusion.1), channel_id=1, replica_groups=mesh['samp'=8,'term'=16] {'samp'}, use_global_device_ids=true, to_apply=%region_9.13 | all-reduce | flops 4096 | bytes 16384 | tf_op jit(solution)/shard_map/psum | solution.py:95
  287.1 36.1 %all-reduce.7.cloned.1.call-done = f32[64,4096]{1,0:T(8,128)} async-done(((f32[64,4096]{1,0:T(8,128)}), f32[64,4096]{1,0:T(8,128)}) %all-reduce.7.cloned.1.call-update) | async-done | bytes 1048592 | tf_op jit(solution)/shard_map/psum | solution.py:101
  325.5 16.9 %convolution_subtract_fusion.1 = f32[1024,4096]{1,0:T(8,128)S(1)} fusion(f32[1024,4096]{1,0:T(8,128)} %gather_fusion.1, f32[1024,64]{0,1:T(8,128)S(1)} %convolution_bitcast_fusion.2, f32[64,4096]{1,0:T(8,128)S(1)} %fusion.19), kind=kOutput, calls=%fused_computation.4 | convolution fusion | flops 3225419776 | bytes 34865152 | tf_op jit(solution)/shard_map/dot_general | solution.py:30
  342.4 5.7 copy-done.2
  348.1 11.1 %fusion.65 = f32[64,4096]{1,0:T(8,128)} fusion(f32[1024,64]{0,1:T(8,128)S(1)} %convolution_subtract_fusion.3, f32[1024,4096]{1,0:T(8,128)S(1)} %convolution_subtract_fusion.1), kind=kOutput, calls=%fused_computation.129 | convolution fusion | flops 3221225472 | bytes 18087936 | tf_op jit(solution)/shard_map/dot_general | solution.py:20
  359.3 9.6 %fusion.6 = bf16[4096,256]{1,0:T(8,128)(2,1)} fusion(bf16[1024,256]{1,0:T(8,128)(2,1)S(1)} %copy-done.4, f32[1024,4096]{1,0:T(8,128)} %gather_fusion.1), kind=kOutput, calls=%fused_computation.11 | convolution fusion | flops 2152726528 | bytes 19398656 | tf_op jit(solution)/shard_map/dot_general | solution.py:34
  368.9 12.8 %reduce-scatter.6.cloned.1.call-start = ((), (), s32[]{:S(2)}) async-start(), calls=%async_computation.9 | async-start | bytes 2359296 | tf_op jit(solution)/shard_map/reduce_scatter | solution.py:81
  381.7 9.7 %fusion.9 = bf16[4096,256]{1,0:T(8,128)(2,1)} fusion(bf16[1024,256]{1,0:T(8,128)(2,1)S(1)} %copy-done.4, f32[1024,4096]{1,0:T(8,128)} %copy-done.2), kind=kOutput, calls=%fused_computation.12 | convolution fusion | flops 2152726528 | bytes 19398656 | tf_op jit(solution)/shard_map/dot_general | solution.py:34
  391.8 23.6 %psum.103 = f32[64,64]{0,1:T(8,128)S(1)} all-reduce(f32[64,64]{0,1:T(8,128)S(1)} %fusion.64), channel_id=1, replica_groups=mesh['samp'=8,'term'=16] {'samp'}, use_global_device_ids=true, to_apply=%region_10.14 | all-reduce | flops 4096 | bytes 32768 | tf_op jit(solution)/shard_map/psum | solution.py:101
  415.5 5.8 cholesky.70
  422.7 4.9 custom-call.14
  428.0 3.2 fusion.17
  431.3 17.0 %convolution_subtract_fusion = f32[1024,4096]{1,0:T(8,128)S(1)} fusion(f32[1024,4096]{1,0:T(8,128)} %copy-done.2, f32[1024,64]{0,1:T(8,128)S(1)} %convolution_bitcast_fusion.1, f32[64,4096]{1,0:T(8,128)} %fusion.17), kind=kOutput, calls=%fused_computation.3 | convolution fusion | flops 3225419776 | bytes 34865152 | tf_op jit(solution)/shard_map/dot_general | solution.py:30
  448.3 5.7 copy-done.3
  454.0 4.0 fusion.12
  458.4 23.7 %psum.106 = bf16[128,64]{1,0:T(8,128)(2,1)S(1)} all-reduce(bf16[128,64]{1,0:T(8,128)(2,1)S(1)} %convolution_convert_fusion), channel_id=1, replica_groups=mesh['samp'=8,'term'=16] {'samp'}, use_global_device_ids=true, to_apply=%region_13.17 | all-reduce | flops 8192 | bytes 32768 | tf_op jit(solution)/shard_map/psum | solution.py:95
  483.8 14.8 %fusion.67 = f32[64,4096]{1,0:T(8,128)} fusion(f32[1024,64]{0,1:T(8,128)S(1)} %convolution_subtract_fusion.2, f32[1024,4096]{1,0:T(8,128)} %copy-done.3), kind=kOutput, calls=%fused_computation.131 | convolution fusion | flops 3221225472 | bytes 18087936 | tf_op jit(solution)/shard_map/dot_general | solution.py:20
  501.1 24.2 %reduce-scatter.8.cloned.1.call-done = bf16[512,256]{1,0:T(8,128)(2,1)} async-done(((bf16[4096,256]{1,0:T(8,128)(2,1)}), bf16[512,256]{1,0:T(8,128)(2,1)}) %reduce-scatter.8.cloned.1.call-update) | async-done | bytes 262160 | tf_op jit(solution)/shard_map/reduce_scatter | solution.py:81
  526.6 24.8 %all-reduce = (f32[64,64]{0,1:T(8,128)S(1)}, f32[4]{0:T(128)S(1)}, f32[4]{0:T(128)S(1)}, f32[4]{0:T(128)S(1)}) all-reduce(f32[64,64]{0,1:T(8,128)S(1)} %fusion.66, f32[4]{0:T(128)S(1)} %reduce_sum.56, f32[4]{0:T(128)S(1)} %reduce_sum.44, f32[4]{0:T(128)S(1)} %reduce_sum.38), channel_id=1, replica_groups=mesh['samp'=8,'term'=16] {'samp'}, use_global_device_ids=true, to_apply=%region_14.18 | all-reduce | flops 4108 | bytes 32864 | tf_op jit(solution)/shard_map/psum | solution.py:101
  551.5 5.8 cholesky.81
  558.7 4.9 custom-call.16
  564.1 27.0 %all-reduce.11.cloned.1.call-done = f32[64,4096]{1,0:T(8,128)} async-done(((f32[64,4096]{1,0:T(8,128)}), f32[64,4096]{1,0:T(8,128)}) %all-reduce.11.cloned.1.call-update) | async-done | bytes 1048592 | tf_op jit(solution)/shard_map/psum | solution.py:101
  593.4 13.9 %fusion.68 = f32[1024,4096]{1,0:T(8,128)S(1)} fusion(f32[1024,64]{0,1:T(8,128)S(1)} %convolution_bitcast_fusion, f32[64,4096]{1,0:T(8,128)S(1)} %fusion.15), kind=kOutput, calls=%fused_computation.132 | convolution fusion | flops 3221225472 | bytes 18087936 | tf_op jit(solution)/shard_map/dot_general | solution.py:30
  (107 shorter events, 37.7 us)
Async XLA Ops:
  7.2 2.9 copy-start
  7.2 30.6 %copy-start.9 = (s32[8192]{0:T(1024)S(1)}, s32[8192]{0:T(1024)}, u32[]{:S(2)}) copy-start(s32[8192]{0:T(1024)} %param.11) | copy-start | bytes 98308
  12.0 21.9 %all-to-all-start = ((f32[8,8,4096]{2,1,0:T(8,128)}), f32[8,8,4096]{2,1,0:T(8,128)S(1)}, u32[]{:S(2)}, u32[]{:S(2)}) async-start(f32[8,8,4096]{2,1,0:T(8,128)} %bitcast), calls=%async_computation | async-start | bytes 2097152 | tf_op jit(solution)/shard_map/all_to_all | solution.py:60
  18.8 97.5 %all-reduce.13.cloned.1.call-start = ((), (), s32[]{:S(2)}) async-start(), calls=%async_computation.11 | async-start | bytes 786432 | tf_op jit(solution)/shard_map/psum | solution.py:16
  31.7 199.4 %all-gather.2.cloned.1.call-start = ((), (), s32[]{:S(2)}) async-start(), calls=%async_computation.4 | async-start | bytes 17825792 | tf_op jit(solution)/shard_map/all_gather | solution.py:63
  33.9 1.0 copy-start.5
  34.9 288.4 %all-reduce.7.cloned.1.call-start = ((), (), s32[]{:S(2)}) async-start(), calls=%async_computation.5 | async-start | bytes 2097152 | tf_op jit(solution)/shard_map/psum | solution.py:101
  152.9 98.5 %copy-start.6 = (bf16[1024,64]{0,1:T(8,128)(2,1)S(1)}, bf16[1024,64]{0,1:T(8,128)(2,1)}, u32[]{:S(2)}) copy-start(bf16[1024,64]{0,1:T(8,128)(2,1)} %get-tuple-element.12) | copy-start | bytes 393220
  251.5 11.7 %copy-start.7 = (bf16[1024,64]{0,1:T(8,128)(2,1)S(1)}, bf16[1024,64]{0,1:T(8,128)(2,1)}, u32[]{:S(2)}) copy-start(bf16[1024,64]{0,1:T(8,128)(2,1)} %get-tuple-element.13) | copy-start | bytes 393220
  262.7 165.4 %all-reduce.9.cloned.1.call-start = ((), (), s32[]{:S(2)}) async-start(), calls=%async_computation.6 | async-start | bytes 2097152 | tf_op jit(solution)/shard_map/psum | solution.py:101
  342.4 5.7 copy-start.2
  348.1 11.2 %copy-start.4 = (bf16[1024,256]{1,0:T(8,128)(2,1)S(1)}, bf16[1024,256]{1,0:T(8,128)(2,1)}, u32[]{:S(2)}) copy-start(bf16[1024,256]{1,0:T(8,128)(2,1)} %param.9) | copy-start | bytes 1572868
  359.2 139.4 %reduce-scatter.4.cloned.1.call-start = ((), (), s32[]{:S(2)}) async-start(), calls=%async_computation.8 | async-start | bytes 2359296 | tf_op jit(solution)/shard_map/reduce_scatter | solution.py:81
  368.9 131.0 %reduce-scatter.6.cloned.1.call-start = ((), (), s32[]{:S(2)}) async-start(), calls=%async_computation.9 | async-start | bytes 2359296 | tf_op jit(solution)/shard_map/reduce_scatter | solution.py:81
  391.4 134.0 %reduce-scatter.8.cloned.1.call-start = ((), (), s32[]{:S(2)}) async-start(), calls=%async_computation.10 | async-start | bytes 2359296 | tf_op jit(solution)/shard_map/reduce_scatter | solution.py:81
  448.2 5.7 copy-start.3
  454.0 4.1 copy-start.8
  458.0 133.1 %all-reduce.11.cloned.1.call-start = ((), (), s32[]{:S(2)}) async-start(), calls=%async_computation.7 | async-start | bytes 2097152 | tf_op jit(solution)/shard_map/psum | solution.py:101
  483.8 127.2 %copy-start.1 = (f32[64,4096]{1,0:T(8,128)S(1)}, f32[64,4096]{1,0:T(8,128)}, u32[]{:S(2)}) copy-start(f32[64,4096]{1,0:T(8,128)} %param.10) | copy-start | bytes 3145732
Sparse Core Ops, SparseCore 0:
  31.8 84.4 all-reduce.12
  118.9 112.0 all-gather.1
  262.8 60.4 all-reduce.6
  359.3 61.9 all-reduce.8
  423.6 31.8 reduce-scatter.3
  457.7 32.5 reduce-scatter.5
  492.8 32.5 reduce-scatter.7
  528.3 62.7 all-reduce.10
where the time goes:
time: 628 us; the launch traced here: 618 us
  waiting for transfers between devices  216 us (34%)
  matrix products  120 us (19%)
  blocking collectives  119 us (19%)
  local copies, waits for them, and re-layouts  70.8 us (11%)
  other arithmetic  49.7 us (8%)
  between operations  23.1 us (4%)
  starting transfers between devices  19.8 us (3%)
    all_gather x1, waiting for transfers between devices, local(): gathered = lax.all_gather(arrived, 'term', axis=0, tiled=True)  78.1 us
    psum x3, blocking collectives, local(): lax.psum((contract(picked, picked), contract(picked, residual)), 'samp')  71.7 us
    psum x3, waiting for transfers between devices, local(): lax.psum((contract(picked, picked), contract(picked, residual)), 'samp')  63.2 us
    dot_general x5, matrix products, product(): jnp.dot(first_arg, second_arg, precision=highest, preferred_element_type=...  48.6 us
    psum x1, waiting for transfers between devices, from_root(): return lax.psum(jnp.where(mine, shard, jnp.zeros_like(shard)), axis)  48 us
    psum x2, blocking collectives, local(): lax.psum(contract(basis_kept, picked).astype(jnp.bfloat16), 'samp')  47 us
    dot_general x8, matrix products, contract(): lax.dot_general(first_arg, second_arg, (((0,), (0,)), ((), ())), precisio...  39.6 us
    scatter x1, local copies, waits for them, and re-layouts, local(): inverse = jnp.zeros((samp_rows,), jnp.int32).at[target_slot.reshape(-1)]....  30.4 us
  transfers between devices with their start and end apart: 9, of which 6 were waited for; matrix products, arithmetic and copies ran while one was open for 23% of the time, Pallas kernels for 0%

commit v1 on v0

v1 whole, which is shorter than its diff:
```python
import functools

import jax
import jax.numpy as jnp
from jax import lax
from jax.experimental import pallas as pl
from jax.experimental.pallas import tpu as pltpu
from jax.sharding import PartitionSpec as P

BLOCK = 64
STEPS = 3
EPS = 1e-06
MESH = pl.DeviceIdType.MESH
HIGHEST = lax.Precision.HIGHEST
F32 = jnp.float32
BF16 = jnp.bfloat16


def nn(a, b, precision=None):
    return lax.dot_general(
        a, b, (((1,), (0,)), ((), ())), precision=precision, preferred_element_type=F32
    )


def nt(a, b, precision=None):
    return lax.dot_general(
        a, b, (((1,), (1,)), ((), ())), precision=precision, preferred_element_type=F32
    )


def tn(a, b):
    return lax.dot_general(a, b, (((0,), (0,)), ((), ())), preferred_element_type=F32)


def iota(shape, dim):
    return lax.broadcasted_iota(jnp.int32, shape, dim)


def ones_where(mask):
    return jnp.where(mask, 1.0, 0.0).astype(BF16)


def split(v):
    hi = v.astype(BF16)
    return hi, (v - hi.astype(F32)).astype(BF16)


def inverse_factor(a):
    n = a.shape[0]
    rows, cols = iota((n, n), 0), iota((n, n), 1)
    inv = jnp.where(rows == cols, 1.0, 0.0).astype(F32)
    below = iota((n, 1), 0)
    for j in range(n - 1):
        scale = 1.0 / a[j : j + 1, j : j + 1]
        col = jnp.where(below > j, a[:, j : j + 1], 0.0) * scale
        a, inv = a - col * a[j : j + 1, :], inv - col * inv[j : j + 1, :]
    diag = jnp.sum(jnp.where(rows == cols, a, 0.0), axis=1, keepdims=True)
    return inv / jnp.sqrt(diag)


def body(
    dims, chosen, index, place, basis, strain, residual, coefs, scores,
    ptp, prs, psum, pry, ptf, sorted4, r1, pit, btg, rg, lo, rlo, pa,
    g_in, g_r, g_z, g_out, x_in, x_r, x_z, x_out, h_in, h_r, h_s, h_z,
    c_own, c_send, c_r, c_s, c_z, c_fin, cg, sg, ss, rs,
):
    rk, slab, tslab, bl = dims
    nr, q4, sr = 128 * rk, 32 * rk, 8 * rk
    p3, p2 = 3 * bl, 2 * bl
    half, group = 2 * tslab, tslab // 2
    total = 8 * nr
    s, t = lax.axis_index("samp"), lax.axis_index("term")
    z, c = s // 2, lax.rem(s, 2)
    y, x = t // 4, lax.rem(t, 4)
    me = s * 4 + x

    def at_x(d):
        return (s, y * 4 + lax.rem(x + d, 4))

    def at_y(d):
        return (s, lax.rem(y + d, 4) * 4 + x)

    def at_z(d):
        return (lax.rem(z + d, 4) * 2 + c, t)

    partner = (z * 2 + 1 - c, t)

    used = [0]

    def sems(n):
        used[0] += n
        return used[0] - n

    def copy(src, dst, k, dev):
        return pltpu.make_async_remote_copy(
            src_ref=src, dst_ref=dst, send_sem=ss.at[k], recv_sem=rs.at[k],
            device_id=dev, device_id_type=MESH,
        )

    def start(copies):
        for one in copies:
            one.start()
        return copies

    def wait_recv(copies):
        for one in copies:
            one.wait_recv()

    pending = []

    def go(copies):
        pending.extend(copies)
        return start(copies)

    def peer(p):
        other = lax.rem(me + p, 32)
        return other // 4, lax.rem(other, 4)

    barrier = pltpu.get_barrier_semaphore()

    def greet(p, carry):
        ps, px = peer(p)
        pl.semaphore_signal(
            barrier, inc=1, device_id=(ps, y * 4 + px), device_id_type=MESH
        )
        return carry

    lax.fori_loop(1, 32, greet, 0)
    for d in (1, 2, 3):
        pl.semaphore_signal(barrier, inc=1, device_id=at_y(d), device_id_type=MESH)

    rows = iota((p3, tslab), 0)
    which = jnp.where(rows < bl, chosen[0], jnp.where(rows < p2, chosen[1], chosen[2]))
    target = which * bl + lax.rem(rows, bl) - t * tslab
    select = ones_where(iota((p3, tslab), 1) == target)
    for q in range(4):
        ptp[q] = nt(select, basis[q * q4 : (q + 1) * q4, :]).astype(BF16)

    order = ones_where(iota((sr, sr), 0) == place[...])

    def sort_slab(j, carry):
        for k in range(4):
            at = pl.multiple_of((j * 4 + k) * slab, slab)
            v = strain[:, pl.ds(at, slab)]
            hi, rest = split(v)
            mid, low = split(v - hi.astype(F32))
            sorted4[j, k] = nn(order, hi) + nn(order, mid) + nn(order, low)
        return carry

    lax.fori_loop(0, 4, sort_slab, 0)

    pl.semaphore_wait(barrier, 34)

    k = sems(3)
    p_x = go([copy(ptp.at[lax.rem(x + d, 4)], prs.at[d - 1], k + d - 1, at_x(d)) for d in (1, 2, 3)])

    ka = sems(1)

    def scatter(p, carry):
        ps, px = peer(p)
        copy(
            sorted4.at[:, px, pl.ds(pl.multiple_of(ps * rk, rk), rk), :],
            r1.at[:, pl.ds(pl.multiple_of(me * rk, rk), rk), :],
            ka,
            (ps, y * 4 + px),
        ).start()
        return carry

    lax.fori_loop(1, 32, scatter, 0)
    for j in range(4):
        r1[j, pl.ds(pl.multiple_of(me * rk, rk), rk), :] = sorted4[
            j, x, pl.ds(pl.multiple_of(s * rk, rk), rk), :
        ]

    def build(q, carry):
        at = pl.multiple_of(q * q4, q4)
        pit[pl.ds(at, q4), :] = ones_where(iota((q4, nr), 0) + at == index[...])
        return carry

    lax.fori_loop(0, 4, build, 0)
    eye = ones_where(iota((tslab, tslab), 0) == iota((tslab, tslab), 1))
    bt = nt(eye, basis[...]).astype(BF16)
    mine = pl.ds(pl.multiple_of(x * tslab, tslab), tslab)
    btg[mine, :] = nn(bt, pit[...]).astype(BF16)

    def ring(ref, view, at, dev, k):
        here, left, right = view(ref, at, None), view(ref, lax.rem(at + 3, 4), 0), view(ref, lax.rem(at + 1, 4), 1)
        first = [copy(here, here, k, dev(1)), copy(here, here, k + 1, dev(3))]
        second = [copy(left, left, k + 2, dev(1)), copy(right, right, k + 3, dev(3))]
        return first, second

    def view_b(ref, slot, part):
        if part is None:
            return ref.at[pl.ds(pl.multiple_of(slot * tslab, tslab), tslab), :]
        return ref.at[pl.ds(pl.multiple_of(slot * tslab + part * group, group), group), :]

    def view_r(ref, slot, part):
        rows = pl.ds(pl.multiple_of(slot * q4, q4), q4)
        if part is None:
            return ref.at[:, rows, :]
        return ref.at[2 * part : 2 * part + 2, rows, :]

    b_first, b_second = ring(btg, view_b, x, at_x, sems(4))
    go(b_first)

    wait_recv(p_x)
    psum[...] = ptp[x] + prs[0] + (prs[1] + prs[2])
    k = sems(3)
    p_y = go([copy(psum, pry.at[d - 1], k + d - 1, at_y(d)) for d in (1, 2, 3)])
    wait_recv(p_y)
    ptf[x] = psum[...] + pry[0] + (pry[1] + pry[2])
    k = sems(3)
    p_g = go([copy(ptf.at[x], ptf.at[x], k + d - 1, at_x(d)) for d in (1, 2, 3)])

    pltpu.make_async_copy(
        r1.at[:, pl.ds(0, 31 * rk), :], r1.at[:, pl.ds(0, 31 * rk), :], rs.at[ka]
    ).wait()
    own_rows = pl.ds(pl.multiple_of(y * q4, q4), q4)

    def halves(j, carry):
        hi, low = split(r1[j])
        rg[j, own_rows, :] = hi
        lo[j] = low
        return carry

    lax.fori_loop(0, 4, halves, 0)
    r_first, r_second = ring(rg, view_r, y, at_y, sems(4))
    go(r_first)
    k = sems(3)
    lows = go([copy(lo.at[lax.rem(y + d, 4)], rlo.at[own_rows, :], k + d - 1, at_y(d)) for d in (1, 2, 3)])
    rlo[own_rows, :] = lo[y]

    b_first[0].wait_recv()
    go(b_second[:1])
    b_first[1].wait_recv()
    go(b_second[1:])

    def reduce_pair(src, got, k):
        return go([copy(src.at[1 - c], got, k, partner)])

    def reduce_ring(src, got, parts, k, pair):
        wait_recv(pair)
        parts[z] = src[c] + got[...]
        return go([copy(parts.at[z], parts.at[z], k + d - 1, at_z(d)) for d in (1, 2, 3)])

    def reduce_back(parts, out, k, around):
        wait_recv(around)
        out[c] = (parts[0] + parts[1]) + (parts[2] + parts[3])
        return go([copy(out.at[c], out.at[c], k, partner)])

    wait_recv(p_g)
    at = 0
    for i in range(3):
        for j in range(i + 1):
            acc = None
            for q in range(4):
                one = nt(ptf[q, i * bl : (i + 1) * bl, :], ptf[q, j * bl : (j + 1) * bl, :])
                acc = one if acc is None else acc + one
            g_in[at // 3, at % 3] = acc
            at += 1
    g_1 = reduce_pair(g_in, g_r, sems(1))
    acc = None
    for q in range(4):
        one = nn(ptf[q], pit[q * q4 : (q + 1) * q4, :])
        acc = one if acc is None else acc + one
    pa[...] = acc.astype(BF16)
    g_2 = reduce_ring(g_in, g_r, g_z, sems(3), g_1)

    r_first[0].wait_recv()
    go(r_second[:1])
    r_first[1].wait_recv()
    go(r_second[1:])

    g_3 = reduce_back(g_z, g_out, sems(1), g_2)
    wait_recv(b_second)

    hk = sems(1)
    other_half = pl.ds(pl.multiple_of((1 - c) * half, half), half)
    own_half = pl.ds(pl.multiple_of(c * half, half), half)
    h_in[1] = nt(btg[other_half, :], pa[:p2, :])
    h_1 = go([copy(h_in.at[1], h_r, hk, partner)])
    h_in[0] = nt(btg[own_half, :], pa[:p2, :])

    wait_recv(g_3)
    gram = [g_out[i // 3, i % 3] / total for i in range(6)]
    w00 = inverse_factor(gram[0])
    l10, l20 = nt(gram[1], w00, HIGHEST), nt(gram[3], w00, HIGHEST)
    w11 = inverse_factor(gram[2] - nt(l10, l10, HIGHEST))
    l21 = nt(gram[4] - nt(l20, l10, HIGHEST), w11, HIGHEST)
    w22 = inverse_factor(gram[5] - nt(l20, l20, HIGHEST) - nt(l21, l21, HIGHEST))
    w10 = -nn(w11, nn(l10, w00, HIGHEST), HIGHEST)
    w20 = -nn(w22, nn(l20, w00, HIGHEST) + nn(l21, w10, HIGHEST), HIGHEST)
    w21 = -nn(w22, nn(l21, w11, HIGHEST), HIGHEST)
    zero = jnp.zeros((bl, bl), F32)
    w = jnp.concatenate(
        [
            jnp.concatenate([w00, zero, zero], axis=1),
            jnp.concatenate([w10, w11, zero], axis=1),
            jnp.concatenate([w20, w21, w22], axis=1),
        ],
        axis=0,
    )
    eye3 = jnp.where(iota((p3, p3), 0) == iota((p3, p3), 1), 1.0, 0.0).astype(F32)
    wt = nt(eye3, w, HIGHEST)

    wait_recv(h_1)
    h_s[...] = h_in[0] + h_r[...]

    def part(ref, zz, *lead):
        return ref.at[(*lead, pl.ds(pl.multiple_of(zz * group, group), group), slice(None))]

    k = sems(3)
    h_2 = go([copy(part(h_s, lax.rem(z + d, 4)), h_z.at[d - 1], k + d - 1, at_z(d)) for d in (1, 2, 3)])

    wait_recv(r_second)
    wait_recv(lows)
    x_mine = nn(pa[...], rg[y]) + nn(pa[...], rlo[...])
    x_in[0] = x_mine[: p3 // 2]
    x_in[1] = x_mine[p3 // 2 :]
    x_1 = reduce_pair(x_in, x_r, sems(1))

    ck, cz = sems(4), sems(12)
    c_1, c_2 = [], []

    def correlate(j):
        c_send[j] = nn(btg[other_half, :], rg[j]).astype(BF16)
        c_1.append(go([copy(c_send.at[j], c_r.at[j], ck + j, partner)]))
        c_own[j] = nn(btg[own_half, :], rg[j])

    def pass_on(j):
        wait_recv(c_1[j])
        both = c_own[j] + c_r[j].astype(F32)
        c_own[j] = both
        c_s[j] = both.astype(BF16)
        c_2.append(
            go([copy(part(c_s, lax.rem(z + d, 4), j), c_z.at[j, d - 1], cz + 3 * j + d - 1, at_z(d)) for d in (1, 2, 3)])
        )

    correlate(0)
    x_2 = reduce_ring(x_in, x_r, x_z, sems(3), x_1)
    correlate(1)
    pass_on(0)
    correlate(2)
    pass_on(1)
    x_3 = reduce_back(x_z, x_out, sems(1), x_2)
    correlate(3)
    pass_on(2)
    wait_recv(x_3)
    cross = jnp.concatenate([x_out[0], x_out[1]], axis=0) / total
    coef = nn(w, cross, HIGHEST)
    coefs[...] = coef
    cg[y] = coef[:p2].astype(BF16)
    k = sems(3)
    cg_1 = go([copy(cg.at[y], cg.at[y], k + d - 1, at_y(d)) for d in (1, 2, 3)])
    pass_on(3)

    y_hi, y_lo = split(nn(wt, coef, HIGHEST))
    for q in range(4):
        at = slice(q * q4, (q + 1) * q4)
        fitted = tn(ptf[q], y_hi) + tn(ptf[q], y_lo)
        residual[at, :] = nn(pit[at, :], rg[y]) + nn(pit[at, :], rlo[...]) - fitted

    wait_recv(h_2)
    h_all = part(h_s, z)[...] + h_z[0] + (h_z[1] + h_z[2])
    hn = nt(h_all, w[:p2, :p2], HIGHEST).astype(BF16)
    first = jnp.where(iota((group, p2), 1) < bl, hn.astype(F32), 0.0).astype(BF16)
    wait_recv(cg_1)
    sums = [None] * 3
    for j in range(4):
        wait_recv(c_2[j])
        c0 = part(c_own, z, j)[...] + c_z[j, 0].astype(F32) + (c_z[j, 1].astype(F32) + c_z[j, 2].astype(F32))
        for i, v in enumerate((c0, c0 - nn(first, cg[j]), c0 - nn(hn, cg[j]))):
            sums[i] = v * v if sums[i] is None else sums[i] + v * v
    own_group = c * 4 + z
    per = group // bl
    rows8, lanes8 = iota((8, 128), 0), iota((8, 128), 1)
    tile = jnp.zeros((8, 128), F32)
    for i in range(3):
        for b in range(per):
            value = jnp.sum(sums[i][b * bl : (b + 1) * bl, :], axis=(0, 1), keepdims=True)
            spot = (rows8 == i) & (lanes8 == lax.rem(own_group, 2) * per + b)
            tile = jnp.where(spot, value, tile)
    sg[me] = tile
    ks = sems(1)

    def tell(p, carry):
        ps, px = peer(p)
        copy(sg.at[me], sg.at[me], ks, (ps, y * 4 + px)).start()
        return carry

    lax.fori_loop(1, 32, tell, 0)
    pltpu.make_async_copy(sg.at[pl.ds(0, 31)], sg.at[pl.ds(0, 31)], rs.at[ks]).wait()
    out = jnp.zeros((8, 128), F32)
    for i in range(2):
        grp = 2 * x + i
        src = (lax.rem(grp, 4) * 2 + grp // 4) * 4
        for px in range(4):
            out = out + sg[src + px]
    out = jnp.sqrt(out / (bl * 16 * slab) + EPS)
    scores[...] = out[:3, : 2 * per]

    pltpu.make_async_copy(
        r1.at[:, pl.ds(0, 31 * rk), :], r1.at[:, pl.ds(0, 31 * rk), :], ss.at[ka]
    ).wait()
    pltpu.make_async_copy(sg.at[pl.ds(0, 31)], sg.at[pl.ds(0, 31)], ss.at[ks]).wait()
    for one in pending:
        one.wait_send()


def local(dims, basis, strain, route, chosen):
    rk, slab, tslab, bl = dims
    nr, q4, sr = 128 * rk, 32 * rk, 8 * rk
    p3, p2 = 3 * bl, 2 * bl
    half, group = 2 * tslab, tslab // 2
    s, t = lax.axis_index("samp"), lax.axis_index("term")

    routes = route.reshape(128, sr)
    goes = routes // nr
    hit = goes == s
    before = jnp.tril(jnp.ones((sr, sr), jnp.bool_), -1)
    rank = jnp.sum(jnp.where(before[None], hit[:, None, :], False), axis=2)
    slot = hit[:, :, None] & (rank[:, :, None] == jnp.arange(rk)[None, None, :])
    sample = jnp.sum(jnp.where(slot, (routes - goes * nr)[:, :, None], 0), axis=1)
    index = sample.reshape(8, 4, 4, rk).transpose(1, 0, 2, 3).reshape(1, nr)
    own = lax.dynamic_index_in_dim(goes, s * 16 + t, 0, keepdims=False)
    same = (own[:, None] == own[None, :]) & before
    place = (own * rk + jnp.sum(same, axis=1)).reshape(1, sr)

    vmem = pl.BlockSpec(memory_space=pltpu.VMEM)
    scratch = [
        ((4, p3, q4), BF16), ((3, p3, q4), BF16), ((p3, q4), BF16), ((3, p3, q4), BF16), ((4, p3, q4), BF16),
        ((4, 4, sr, slab), F32), ((4, q4, slab), F32), ((nr, nr), BF16), ((4 * tslab, nr), BF16),
        ((4, nr, slab), BF16), ((4, q4, slab), BF16), ((nr, slab), BF16), ((p3, nr), BF16),
        ((2, 3, bl, bl), F32), ((3, bl, bl), F32), ((4, 3, bl, bl), F32), ((2, 3, bl, bl), F32),
        ((2, p3 // 2, slab), F32), ((p3 // 2, slab), F32), ((4, p3 // 2, slab), F32), ((2, p3 // 2, slab), F32),
        ((2, half, p2), F32), ((half, p2), F32), ((half, p2), F32), ((3, group, p2), F32),
        ((4, half, slab), F32), ((4, half, slab), BF16), ((4, half, slab), BF16), ((4, half, slab), BF16),
        ((4, 3, group, slab), BF16), ((8, 128), F32), ((4, p2, slab), BF16), ((32, 8, 128), F32),
    ]
    return pl.pallas_call(
        functools.partial(body, dims),
        out_shape=(
            jax.ShapeDtypeStruct((nr, slab), F32),
            jax.ShapeDtypeStruct((p3, slab), F32),
            jax.ShapeDtypeStruct((3, tslab // bl), F32),
        ),
        in_specs=[pl.BlockSpec(memory_space=pltpu.SMEM), vmem, vmem, vmem, vmem],
        out_specs=(vmem, vmem, vmem),
        scratch_shapes=[pltpu.VMEM(shape, dtype) for shape, dtype in scratch]
        + [pltpu.SemaphoreType.DMA((64,)), pltpu.SemaphoreType.DMA((64,))],
        compiler_params=pltpu.CompilerParams(
            collective_id=0, has_side_effects=True, vmem_limit_bytes=60 * 1024 * 1024
        ),
    )(chosen, index, place, basis, strain)


def solution(mesh, dims=(8, 256, 256, BLOCK)):
    return jax.shard_map(
        functools.partial(local, dims),
        mesh=mesh,
        in_specs=(P("samp", "term"), P(("samp", "term"), None), P(), P()),
        out_specs=(P("samp", "term"), P(None, "term"), P(None, "term")),
        check_vma=False,
    )
```

time: 628 us -> 108 us (0.17); the launches traced: 618 us -> 107 us
  waiting for transfers between devices: 216 us -> 0 us
  matrix products: 120 us -> 0 us
  blocking collectives: 119 us -> 0 us
  Pallas kernels: 0 us -> 99.6 us
  local copies, waits for them, and re-layouts: 70.8 us -> 5.39 us
  other arithmetic: 49.7 us -> 1.73 us
  between operations: 23.1 us -> 0.71 us
  starting transfers between devices: 19.8 us -> 0 us
    psum x5 -> x0, blocking collectives: 119 us -> none  [the longest x3 71.7 us: local(): lax.psum((contract(picked, picked), contract(picked, residual)), 'samp')]
    dot_general x16 -> x0, matrix products: 111 us -> none  [the longest x5 48.6 us: product(): jnp.dot(first_arg, second_arg, precision=highest, preferred_element_type=...]
    psum x4 -> x0, waiting for transfers between devices: 111 us -> none  [the longest x3 63.2 us: local(): lax.psum((contract(picked, picked), contract(picked, residual)), 'samp')]
    pallas_call x0 -> x1, Pallas kernels: none -> 99.6 us  [local(): pl.pallas_call(functools.partial(body, dims), out_shape=(jax.ShapeDtypeSt...]
    all_gather x1 -> x0, waiting for transfers between devices: 78.1 us -> none  [local(): gathered = lax.all_gather(arrived, 'term', axis=0, tiled=True)]
    another operation x20 -> x0, other arithmetic: 38.6 us -> none  [the longest x9 19.6 us: local(): lower_factor = jnp.linalg.cholesky(gram_matrix / total_rows)]
    scatter x1 -> x0, local copies, waits for them, and re-layouts: 30.4 us -> none  [local(): inverse = jnp.zeros((samp_rows,), jnp.int32).at[target_slot.reshape(-1)]....]
    reduce_scatter x3 -> x0, waiting for transfers between devices: 24.3 us -> none  [local(): lax.psum_scatter(make_term(basis, residual.astype(jnp.bfloat16)).astype(j...]
  transfers between devices with their start and end apart: 9 -> 0, of which waited for: 6 -> 0; matrix products, arithmetic and copies ran while one was open for 23% -> 0% of each run, Pallas kernels for 0% -> 0%
where the time goes in v1:
time: 108 us; the launch traced here: 107 us
  Pallas kernels  99.6 us (92%)
  local copies, waits for them, and re-layouts  5.39 us (5%)
  other arithmetic  1.73 us (2%)
    pallas_call x1, Pallas kernels, local(): pl.pallas_call(functools.partial(body, dims), out_shape=(jax.ShapeDtypeSt...  99.6 us
    unnamed x7, local copies, waits for them, and re-layouts  3.56 us

profile of v1, /device:TPU:1, one launch (start us, length us, event | category | flops | bytes accessed | tf_op | source)
XLA Modules:
  0.0 107.4 jit_solution(7715837303556571695)
XLA Ops:
  0.6 0.1 iota_compare_fusion.1
  0.7 0.8 reshape.105
  1.6 0.1 broadcast_compare_fusion
  1.6 0.1 copy.14
  1.7 0.8 convert_reduce_fusion
  2.5 0.1 copy.16
  2.6 0.1 select_reduce_fusion
  2.7 0.2 convert_reduce_fusion.1
  2.9 0.5 bitcast_add_fusion.place
  3.4 0.1 copy.17
  3.5 0.7 reshape.107.index
  4.2 99.6 %shard_map.67 = (f32[1024,256]{1,0:T(8,128)}, f32[192,256]{1,0:T(8,128)}, f32[3,4]{1,0:T(4,128)}) custom-call(s32[3]{0:T(128)} %chosen.1, s32[1,1024]{1,0:T(1,128)} %reshape.107.index, s32[1,64]{1,0:T(1,128)} %bitcast_add_fusion.place, bf16[1024,256]{1,0:T(8,128)(2,1)} %basis.1, f32[64,4096]{1,0:T(8,128)} %strain.1), custom_call_target="tpu_custom_call" | custom-call | tf_op jit(solution)/shard_map/pallas_call | solution.py:440
  103.8 0.0 copy-start
  103.8 0.0 copy-start.1
  103.8 2.3 %copy.23 = f32[1024,256]{1,0:T(8,128)} copy(f32[1024,256]{1,0:T(8,128)} %get-tuple-element.8) | data formatting | bytes 2097152
  106.1 0.0 copy-done
  106.1 0.7 copy.24
  106.8 0.0 copy-done.1
  106.8 0.6 copy.25
  (4 shorter events, 0.1 us)
Async XLA Ops:
  103.8 2.3 %copy-start = (f32[192,256]{1,0:T(8,128)S(1)}, f32[192,256]{1,0:T(8,128)}, u32[]{:S(2)}) copy-start(f32[192,256]{1,0:T(8,128)} %get-tuple-element.9) | copy-start | bytes 589828
  103.8 3.0 %copy-start.1 = (f32[3,4]{1,0:T(4,128)S(1)}, f32[3,4]{1,0:T(4,128)}, u32[]{:S(2)}) copy-start(f32[3,4]{1,0:T(4,128)} %get-tuple-element.10) | copy-start | bytes 148

commit v2 on v1

v2 whole, which is shorter than its diff:
```python
import functools

import jax
import jax.numpy as jnp
from jax import lax
from jax.experimental import pallas as pl
from jax.experimental.pallas import tpu as pltpu
from jax.sharding import PartitionSpec as P

BLOCK = 64
STEPS = 3
EPS = 1e-06
MESH = pl.DeviceIdType.MESH
HIGHEST = lax.Precision.HIGHEST
F32 = jnp.float32
BF16 = jnp.bfloat16


def nn(a, b, precision=None):
    return lax.dot_general(
        a, b, (((1,), (0,)), ((), ())), precision=precision, preferred_element_type=F32
    )


def nt(a, b, precision=None):
    return lax.dot_general(
        a, b, (((1,), (1,)), ((), ())), precision=precision, preferred_element_type=F32
    )


def tn(a, b):
    return lax.dot_general(a, b, (((0,), (0,)), ((), ())), preferred_element_type=F32)


def iota(shape, dim):
    return lax.broadcasted_iota(jnp.int32, shape, dim)


def ones_where(mask):
    return jnp.where(mask, 1.0, 0.0).astype(BF16)


def split(v):
    hi = v.astype(BF16)
    return hi, (v - hi.astype(F32)).astype(BF16)


class Bulk:
    def __init__(self, view, send_sem, recv_sem):
        self.view, self.send_sem, self.recv_sem = view, send_sem, recv_sem

    def wait_send(self):
        pltpu.make_async_copy(self.view, self.view, self.send_sem).wait()

    def wait_recv(self):
        pltpu.make_async_copy(self.view, self.view, self.recv_sem).wait()


def inverse_factor(a, width=8):
    n = a.shape[0]
    width = min(width, n)
    rows, cols = iota((n, n), 0), iota((n, n), 1)
    inv = jnp.where(rows == cols, 1.0, 0.0).astype(F32)
    for g in range(0, n, width):
        picked = range(g, g + width)
        columns = [jnp.broadcast_to(a[:, j : j + 1], (n, n)) for j in picked]
        rows_a = [a[j : j + 1, :] for j in picked]
        rows_i = [inv[j : j + 1, :] for j in picked]
        drop_a = drop_i = 0.0
        for i, j in enumerate(picked):
            scale = 1.0 / columns[i][j : j + 1, :]
            unit_a, unit_i = rows_a[i] * scale, rows_i[i] * scale
            below = jnp.where(rows > j, columns[i], 0.0)
            for m in range(i + 1, width):
                factor = columns[i][g + m : g + m + 1, :]
                rows_a[m] = rows_a[m] - factor * unit_a
                rows_i[m] = rows_i[m] - factor * unit_i
                columns[m] = columns[m] - below * (columns[m][j : j + 1, :] * scale)
            drop_a, drop_i = drop_a + below * unit_a, drop_i + below * unit_i
        a, inv = a - drop_a, inv - drop_i
    diag = jnp.sum(jnp.where(rows == cols, a, 0.0), axis=1, keepdims=True)
    return inv / jnp.sqrt(diag)


def body(
    dims, chosen, index, place, basis, strain, residual, coefs, scores,
    ptp, prs, psum, pry, ptf, out_h, mid_h, in_h, out_l, mid_l, in_l, pit, btg, rg, lo, rlo, pa,
    g_in, g_r, g_z, g_out, x_in, x_r, x_z, x_out, v_in, v_r, v_z, v_out, h_in, h_r, h_s, h_z,
    c_own, c_send, c_r, c_s, c_z, cg, sx, sg, wi, wm, wtm, ss, rs,
):
    rk, slab, tslab, bl = dims
    nr, q4, sr = 128 * rk, 32 * rk, 8 * rk
    p3, p2 = 3 * bl, 2 * bl
    half, group, wide = 2 * tslab, tslab // 2, slab // 2
    total = 8 * nr
    s, t = lax.axis_index("samp"), lax.axis_index("term")
    z, c = s // 2, lax.rem(s, 2)
    y, x = t // 4, lax.rem(t, 4)

    def at_x(d):
        return (s, y * 4 + lax.rem(x + d, 4))

    def at_y(d):
        return (s, lax.rem(y + d, 4) * 4 + x)

    def at_s(d):
        return (lax.rem(s + d, 8), t)

    def at_z(d):
        return (lax.rem(z + d, 4) * 2 + c, t)

    partner = (z * 2 + 1 - c, t)

    used = [0]

    def sems(n):
        used[0] += n
        return used[0] - n

    def copy(src, dst, k, dev):
        return pltpu.make_async_remote_copy(
            src_ref=src, dst_ref=dst, send_sem=ss.at[k], recv_sem=rs.at[k],
            device_id=dev, device_id_type=MESH,
        )

    def start(copies):
        for one in copies:
            one.start()
        return copies

    pending, awaited = [], []

    def wait_recv(copies):
        for one in copies:
            one.wait_recv()
            awaited[:] = [other for other in awaited if other is not one]

    def track(copies):
        pending.extend(copies)
        awaited.extend(copies)
        return copies

    def go(copies):
        return start(track(copies))

    def finish():
        wait_recv(list(awaited))
        for one in pending:
            one.wait_send()

    barrier = pltpu.get_barrier_semaphore()

    def greet(dev):
        pl.semaphore_signal(barrier, inc=1, device_id=dev, device_id_type=MESH)

    for d in (1, 2, 3):
        greet(at_x(d))
        greet(at_y(d))
    for d in range(1, 8):
        greet(at_s(d))

    rows = iota((p3, tslab), 0)
    which = jnp.where(rows < bl, chosen[0], jnp.where(rows < p2, chosen[1], chosen[2]))
    target = which * bl + lax.rem(rows, bl) - t * tslab
    select = ones_where(iota((p3, tslab), 1) == target)
    for q in range(4):
        ptp[q] = nt(select, basis[q * q4 : (q + 1) * q4, :]).astype(BF16)

    order = ones_where(iota((sr, sr), 0) == place[...])

    def packed(v):
        pair = [v[:, n * wide : (n + 1) * wide].reshape(8, rk, wide) for n in (0, 1)]
        return jnp.stack(pair, axis=1).reshape(8, 2 * rk, wide).astype(BF16)

    def unpacked(v):
        v = v.astype(F32).reshape(32, 2, rk, wide)
        return jnp.concatenate([v[:, n].reshape(q4, wide) for n in (0, 1)], axis=1).astype(BF16)

    def sort_slab(j, carry):
        for k in range(4):
            at = pl.multiple_of((j * 4 + k) * slab, slab)
            hi, low = split(strain[:, pl.ds(at, slab)])
            out_h[j, :, k] = packed(nn(order, hi))
            out_l[j, :, k] = packed(nn(order, low))
        return carry

    lax.fori_loop(0, 4, sort_slab, 0)

    pl.semaphore_wait(barrier, 13)

    k = sems(3)
    p_1 = go([copy(ptp.at[lax.rem(y + d, 4)], prs.at[d - 1], k + d - 1, at_y(d)) for d in (1, 2, 3)])

    to_s, to_x = {}, {}

    def send_z(low, j):
        src, dst = ((out_h, mid_h), (out_l, mid_l))[low]
        k = sems(1)

        def scatter(d, carry):
            dev = at_s(d)
            copy(src.at[j, dev[0]], dst.at[j, s], k, dev).start()
            return carry

        lax.fori_loop(1, 8, scatter, 0)
        to_s[low, j] = track([Bulk(dst.at[j, pl.ds(0, 7)], ss.at[k], rs.at[k])])
        dst[j, s] = src[j, s]

    def send_x(low, j):
        src, dst = ((mid_h, in_h), (mid_l, in_l))[low]
        wait_recv(to_s[low, j])
        k = sems(3)
        to_x[low, j] = go([copy(src.at[j, :, lax.rem(x + d, 4)], dst.at[j, x], k + d - 1, at_x(d)) for d in (1, 2, 3)])
        dst[j, x] = src[j, :, x]

    send_z(0, 0)
    send_z(0, 1)

    def build(q, carry):
        at = pl.multiple_of(q * q4, q4)
        pit[pl.ds(at, q4), :] = ones_where(iota((q4, nr), 0) + at == index[...])
        return carry

    lax.fori_loop(0, 4, build, 0)
    eye = ones_where(iota((tslab, tslab), 0) == iota((tslab, tslab), 1))
    bt = nt(eye, basis[...]).astype(BF16)
    btg[pl.ds(pl.multiple_of(x * tslab, tslab), tslab), :] = nn(bt, pit[...]).astype(BF16)

    own_rows = pl.ds(pl.multiple_of(y * q4, q4), q4)
    piece = tslab // 4
    b_out, b_on, r_out, r_on = [], [], [], []

    def b_view(slot, i):
        return btg.at[pl.ds(pl.multiple_of(slot * tslab + i * piece, piece), piece), :]

    def r_view(slot, j):
        return rg.at[j, pl.ds(pl.multiple_of(slot * q4, q4), q4), :]

    def ring_out(view, i, at, dev):
        k = sems(2)
        return go([copy(view(at, i), view(at, i), k + n, dev(1 + 2 * n)) for n in (0, 1)])

    def ring_on(view, i, at, dev, out):
        wait_recv([out[i // 2]])
        slot = lax.rem(at + (3, 1)[i // 2], 4)
        k = sems(1)
        return go([copy(view(slot, i), view(slot, i), k, dev((1, 3)[i // 2]))])

    def send_b(i):
        b_out.append(ring_out(b_view, i, x, at_x))

    def pass_b(i):
        b_on.append(ring_on(b_view, i, x, at_x, b_out[i]))

    def send_r(j):
        wait_recv(to_x[0, j])
        rg[j, own_rows, :] = unpacked(in_h[j])
        r_out.append(ring_out(r_view, j, y, at_y))

    def pass_r(j):
        r_on.append(ring_on(r_view, j, y, at_y, r_out[j]))

    send_b(0)
    send_x(0, 0)
    send_z(0, 2)
    wait_recv(p_1)
    psum[...] = ptp[y] + prs[0] + (prs[1] + prs[2])
    k = sems(3)
    p_2 = go([copy(psum, pry.at[d - 1], k + d - 1, at_x(d)) for d in (1, 2, 3)])
    send_b(1)
    send_x(0, 1)
    send_z(0, 3)
    send_r(0)
    pass_b(0)
    wait_recv(p_2)
    ptf[y] = psum[...] + pry[0] + (pry[1] + pry[2])
    k = sems(3)
    p_3 = go([copy(ptf.at[y], ptf.at[y], k + d - 1, at_y(d)) for d in (1, 2, 3)])
    send_x(0, 2)
    send_z(1, 0)
    send_b(2)
    send_r(1)
    pass_r(0)
    pass_b(1)
    send_x(0, 3)
    send_z(1, 1)
    send_b(3)

    def reduce_pair(src, got, k):
        return go([copy(src.at[1 - c], got, k, partner)])

    def reduce_ring(src, got, parts, k, pair):
        wait_recv(pair)
        parts[z] = src[c] + got[...]
        return go([copy(parts.at[z], parts.at[z], k + d - 1, at_z(d)) for d in (1, 2, 3)])

    def reduce_back(parts, out, k, around):
        wait_recv(around)
        out[c] = (parts[0] + parts[1]) + (parts[2] + parts[3])
        return go([copy(out.at[c], out.at[c], k, partner)])

    wait_recv(p_3)
    at = 0
    for i in range(3):
        for j in range(i + 1):
            acc = None
            for q in range(4):
                one = nt(ptf[q, i * bl : (i + 1) * bl, :], ptf[q, j * bl : (j + 1) * bl, :])
                acc = one if acc is None else acc + one
            g_in[at // 3, at % 3] = acc
            at += 1
    g_1 = reduce_pair(g_in, g_r, sems(1))
    send_r(2)
    pass_r(1)
    pass_b(2)
    g_2 = reduce_ring(g_in, g_r, g_z, sems(3), g_1)
    send_z(1, 2)
    send_z(1, 3)
    acc = None
    for q in range(4):
        one = nn(ptf[q], pit[q * q4 : (q + 1) * q4, :])
        acc = one if acc is None else acc + one
    pa[...] = acc.astype(BF16)
    send_r(3)
    pass_r(2)
    pass_b(3)
    g_3 = reduce_back(g_z, g_out, sems(1), g_2)
    for j in range(4):
        send_x(1, j)
    pass_r(3)

    def lows_on():
        for j in range(4):
            wait_recv(to_x[1, j])
            lo[j] = unpacked(in_l[j])
        k = sems(3)
        rlo[own_rows, :] = lo[y]
        return go([copy(lo.at[lax.rem(y + d, 4)], rlo.at[own_rows, :], k + d - 1, at_y(d)) for d in (1, 2, 3)])

    wait_recv(g_3)

    def factor(i, a):
        wi[i] = inverse_factor(a)

    def rest(i, j):
        return g_out[(i * (i + 1) // 2 + j) // 3, (i * (i + 1) // 2 + j) % 3] / total

    factor(0, rest(0, 0))

    def left_over(copies):
        return [got for got in copies if any(got is other for other in awaited)]

    for i in range(4):
        wait_recv(left_over(b_out[i] + b_on[i]))
    hk = sems(1)
    other_half = pl.ds(pl.multiple_of((1 - c) * half, half), half)
    own_half = pl.ds(pl.multiple_of(c * half, half), half)
    h_in[1] = nt(btg[other_half, :], pa[:p2, :])
    h_1 = go([copy(h_in.at[1], h_r, hk, partner)])
    h_in[0] = nt(btg[own_half, :], pa[:p2, :])

    def part(ref, zz, *lead):
        return ref.at[(*lead, pl.ds(pl.multiple_of(zz * group, group), group), slice(None))]

    ck, cz = sems(4), sems(12)
    c_1, c_2 = [], []

    def correlate(j):
        wait_recv(left_over(r_out[j] + r_on[j]))
        c_send[j] = nn(btg[other_half, :], rg[j]).astype(BF16)
        c_1.append(go([copy(c_send.at[j], c_r.at[j], ck + j, partner)]))
        c_own[j] = nn(btg[own_half, :], rg[j])

    def pass_on(j):
        wait_recv(c_1[j])
        both = c_own[j] + c_r[j].astype(F32)
        c_own[j] = both
        c_s[j] = both.astype(BF16)
        c_2.append(
            go([copy(part(c_s, lax.rem(z + d, 4), j), c_z.at[j, d - 1], cz + 3 * j + d - 1, at_z(d)) for d in (1, 2, 3)])
        )

    correlate(0)
    wait_recv(h_1)
    h_s[...] = h_in[0] + h_r[...]
    k = sems(3)
    h_2 = go([copy(part(h_s, lax.rem(z + d, 4)), h_z.at[d - 1], k + d - 1, at_z(d)) for d in (1, 2, 3)])
    pass_on(0)
    w00 = wi[0]
    l10, l20 = nt(rest(1, 0), w00, HIGHEST), nt(rest(2, 0), w00, HIGHEST)
    factor(1, rest(1, 1) - nt(l10, l10, HIGHEST))
    correlate(1)
    lows = lows_on()
    pass_on(1)
    correlate(2)
    w11 = wi[1]
    l21 = nt(rest(2, 1) - nt(l20, l10, HIGHEST), w11, HIGHEST)
    factor(2, rest(2, 2) - nt(l20, l20, HIGHEST) - nt(l21, l21, HIGHEST))
    pass_on(2)
    for j in range(4):
        wait_recv(left_over(r_out[j] + r_on[j]))

    def cross_pair(v, src, got):
        src[0] = v[: p3 // 2]
        src[1] = v[p3 // 2 :]
        return reduce_pair(src, got, sems(1))

    x_1 = cross_pair(nn(pa[...], rg[y]), x_in, x_r)
    correlate(3)
    x_2 = reduce_ring(x_in, x_r, x_z, sems(3), x_1)
    pass_on(3)
    w22 = wi[2]
    w10 = -nn(w11, nn(l10, w00, HIGHEST), HIGHEST)
    w20 = -nn(w22, nn(l20, w00, HIGHEST) + nn(l21, w10, HIGHEST), HIGHEST)
    w21 = -nn(w22, nn(l21, w11, HIGHEST), HIGHEST)
    zero = jnp.zeros((bl, bl), F32)
    wm[...] = jnp.concatenate(
        [
            jnp.concatenate([w00, zero, zero], axis=1),
            jnp.concatenate([w10, w11, zero], axis=1),
            jnp.concatenate([w20, w21, w22], axis=1),
        ],
        axis=0,
    )
    x_3 = reduce_back(x_z, x_out, sems(1), x_2)
    eye3 = jnp.where(iota((p3, p3), 0) == iota((p3, p3), 1), 1.0, 0.0).astype(F32)
    wtm[...] = nt(eye3, wm[...], HIGHEST)
    wait_recv(x_3)
    cross = jnp.concatenate([x_out[0], x_out[1]], axis=0) / total
    coef = nn(wm[:p2, :p2], cross[:p2], HIGHEST)
    cg[y] = coef.astype(BF16)
    k = sems(3)
    cg_1 = go([copy(cg.at[y], cg.at[y], k + d - 1, at_y(d)) for d in (1, 2, 3)])
    wait_recv(lows)
    v_1 = cross_pair(nn(pa[...], rlo[...]), v_in, v_r)
    for q in range(2):
        at = slice(q * q4, (q + 1) * q4)
        residual[at, :] = nn(pit[at, :], rg[y]) + nn(pit[at, :], rlo[...])
    v_2 = reduce_ring(v_in, v_r, v_z, sems(3), v_1)
    for q in range(2, 4):
        at = slice(q * q4, (q + 1) * q4)
        residual[at, :] = nn(pit[at, :], rg[y]) + nn(pit[at, :], rlo[...])

    def settle():
        wait_recv(v_3)
        low = jnp.concatenate([v_out[0], v_out[1]], axis=0) / total
        coef = nn(wm[...], cross + low, HIGHEST)
        coefs[...] = coef
        y_hi, y_lo = split(nn(wtm[...], coef, HIGHEST))
        for q in range(4):
            at = slice(q * q4, (q + 1) * q4)
            residual[at, :] = residual[at, :] - (tn(ptf[q], y_hi) + tn(ptf[q], y_lo))

    wait_recv(h_2)
    h_all = part(h_s, z)[...] + h_z[0] + (h_z[1] + h_z[2])
    hn = nt(h_all, wm[:p2, :p2], HIGHEST).astype(BF16)
    first = jnp.where(iota((group, p2), 1) < bl, hn.astype(F32), 0.0).astype(BF16)
    wait_recv(cg_1)
    sums = [None] * 3
    for j in range(4):
        wait_recv(c_2[j])
        c0 = part(c_own, z, j)[...] + c_z[j, 0].astype(F32) + (c_z[j, 1].astype(F32) + c_z[j, 2].astype(F32))
        for i, v in enumerate((c0, c0 - nn(first, cg[j]), c0 - nn(hn, cg[j]))):
            sums[i] = v * v if sums[i] is None else sums[i] + v * v
    own_group = c * 4 + z
    per = group // bl
    rows8, lanes8 = iota((8, 128), 0), iota((8, 128), 1)
    tile = jnp.zeros((8, 128), F32)
    for i in range(3):
        for b in range(per):
            value = jnp.sum(sums[i][b * bl : (b + 1) * bl, :], axis=(0, 1), keepdims=True)
            spot = (rows8 == i) & (lanes8 == lax.rem(own_group, 2) * per + b)
            tile = jnp.where(spot, value, tile)
    sx[x] = tile
    v_3 = reduce_back(v_z, v_out, sems(1), v_2)
    k = sems(3)
    s_1 = go([copy(sx.at[x], sx.at[x], k + d - 1, at_x(d)) for d in (1, 2, 3)])
    settle()
    wait_recv(s_1)
    sg[s] = (sx[0] + sx[1]) + (sx[2] + sx[3])
    ks = sems(1)

    def tell(d, carry):
        copy(sg.at[s], sg.at[s], ks, at_s(d)).start()
        return carry

    lax.fori_loop(1, 8, tell, 0)
    wait_recv(track([Bulk(sg.at[pl.ds(0, 7)], ss.at[ks], rs.at[ks])]))
    out = jnp.zeros((8, 128), F32)
    for i in range(2):
        grp = 2 * x + i
        out = out + sg[lax.rem(grp, 4) * 2 + grp // 4]
    out = jnp.sqrt(out / (bl * 16 * slab) + EPS)
    scores[...] = out[:3, : 2 * per]

    finish()


def local(dims, basis, strain, route, chosen):
    rk, slab, tslab, bl = dims
    nr, q4, sr = 128 * rk, 32 * rk, 8 * rk
    p3, p2 = 3 * bl, 2 * bl
    half, group = 2 * tslab, tslab // 2
    s, t = lax.axis_index("samp"), lax.axis_index("term")

    routes = route.reshape(128, sr)
    goes = routes // nr
    hit = goes == s
    before = jnp.tril(jnp.ones((sr, sr), jnp.bool_), -1)
    rank = jnp.sum(jnp.where(before[None], hit[:, None, :], False), axis=2)
    slot = hit[:, :, None] & (rank[:, :, None] == jnp.arange(rk)[None, None, :])
    sample = jnp.sum(jnp.where(slot, (routes - goes * nr)[:, :, None], 0), axis=1)
    index = sample.reshape(8, 4, 4, rk).transpose(1, 2, 0, 3).reshape(1, nr)
    own = lax.dynamic_index_in_dim(goes, s * 16 + t, 0, keepdims=False)
    same = (own[:, None] == own[None, :]) & before
    place = (own * rk + jnp.sum(same, axis=1)).reshape(1, sr)

    vmem = pl.BlockSpec(memory_space=pltpu.VMEM)
    scratch = [
        ((4, p3, q4), BF16), ((3, p3, q4), BF16), ((p3, q4), BF16), ((3, p3, q4), BF16), ((4, p3, q4), BF16),
        *[((4, 8, 4, 2 * rk, slab // 2), BF16), ((4, 8, 4, 2 * rk, slab // 2), BF16), ((4, 4, 8, 2 * rk, slab // 2), BF16)] * 2,
        ((nr, nr), BF16), ((4 * tslab, nr), BF16),
        ((4, nr, slab), BF16), ((4, q4, slab), BF16), ((nr, slab), BF16), ((p3, nr), BF16),
        ((2, 3, bl, bl), F32), ((3, bl, bl), F32), ((4, 3, bl, bl), F32), ((2, 3, bl, bl), F32),
        *[((2, p3 // 2, slab), F32), ((p3 // 2, slab), F32), ((4, p3 // 2, slab), F32), ((2, p3 // 2, slab), F32)] * 2,
        ((2, half, p2), F32), ((half, p2), F32), ((half, p2), F32), ((3, group, p2), F32),
        ((4, half, slab), F32), ((4, half, slab), BF16), ((4, half, slab), BF16), ((4, half, slab), BF16),
        ((4, 3, group, slab), BF16), ((4, p2, slab), BF16), ((4, 8, 128), F32), ((8, 8, 128), F32),
        ((3, bl, bl), F32), ((p3, p3), F32), ((p3, p3), F32),
    ]
    return pl.pallas_call(
        functools.partial(body, dims),
        out_shape=(
            jax.ShapeDtypeStruct((nr, slab), F32),
            jax.ShapeDtypeStruct((p3, slab), F32),
            jax.ShapeDtypeStruct((3, tslab // bl), F32),
        ),
        in_specs=[pl.BlockSpec(memory_space=pltpu.SMEM), vmem, vmem, vmem, vmem],
        out_specs=(vmem, vmem, vmem),
        scratch_shapes=[pltpu.VMEM(shape, dtype) for shape, dtype in scratch]
        + [pltpu.SemaphoreType.DMA((128,)), pltpu.SemaphoreType.DMA((128,))],
        compiler_params=pltpu.CompilerParams(
            collective_id=0, has_side_effects=True, vmem_limit_bytes=60 * 1024 * 1024
        ),
    )(chosen, index, place, basis, strain)


def solution(mesh, dims=(8, 256, 256, BLOCK)):
    return jax.shard_map(
        functools.partial(local, dims),
        mesh=mesh,
        in_specs=(P("samp", "term"), P(("samp", "term"), None), P(), P()),
        out_specs=(P("samp", "term"), P(None, "term"), P(None, "term")),
        check_vma=False,
    )
```

time: 108 us -> 95.2 us (0.88)
  Pallas kernels: 99.6 us -> 87.1 us
    pallas_call x1, Pallas kernels: 99.6 us -> 87.1 us  [local(): pl.pallas_call(functools.partial(body, dims), out_shape=(jax.ShapeDtypeSt...]
where the time goes in v2:
time: 95.2 us; the launch traced here: 95 us
  Pallas kernels  87.1 us (91%)
  local copies, waits for them, and re-layouts  5.38 us (6%)
  other arithmetic  1.73 us (2%)
    pallas_call x1, Pallas kernels, local(): pl.pallas_call(functools.partial(body, dims), out_shape=(jax.ShapeDtypeSt...  87.1 us
    unnamed x7, local copies, waits for them, and re-layouts  3.56 us

profile of v2, /device:TPU:1, one launch (start us, length us, event | category | flops | bytes accessed | tf_op | source)
XLA Modules:
  0.0 95.0 jit_solution(5217299523171563769)
XLA Ops:
  0.6 0.1 iota_compare_fusion.1
  0.7 0.8 reshape.105
  1.6 0.1 broadcast_compare_fusion
  1.6 0.1 copy.14
  1.7 0.8 convert_reduce_fusion
  2.5 0.1 copy.16
  2.6 0.1 select_reduce_fusion
  2.7 0.2 convert_reduce_fusion.1
  2.9 0.5 bitcast_add_fusion.place
  3.4 0.1 copy.17
  3.5 0.7 reshape.107.index
  4.2 87.1 %shard_map.67 = (f32[1024,256]{1,0:T(8,128)}, f32[192,256]{1,0:T(8,128)}, f32[3,4]{1,0:T(4,128)}) custom-call(s32[3]{0:T(128)} %chosen.1, s32[1,1024]{1,0:T(1,128)} %reshape.107.index, s32[1,64]{1,0:T(1,128)} %bitcast_add_fusion.place, bf16[1024,256]{1,0:T(8,128)(2,1)} %basis.1, f32[64,4096]{1,0:T(8,128)} %strain.1), custom_call_target="tpu_custom_call" | custom-call | tf_op jit(solution)/shard_map/pallas_call | solution.py:531
  91.4 0.0 copy-start
  91.4 0.0 copy-start.1
  91.4 2.3 %copy.23 = f32[1024,256]{1,0:T(8,128)} copy(f32[1024,256]{1,0:T(8,128)} %get-tuple-element.8) | data formatting | bytes 2097152
  93.7 0.0 copy-done
  93.7 0.7 copy.24
  94.4 0.0 copy-done.1
  94.4 0.6 copy.25
  (4 shorter events, 0.1 us)
Async XLA Ops:
  91.4 2.3 %copy-start = (f32[192,256]{1,0:T(8,128)S(1)}, f32[192,256]{1,0:T(8,128)}, u32[]{:S(2)}) copy-start(f32[192,256]{1,0:T(8,128)} %get-tuple-element.9) | copy-start | bytes 589828
  91.4 3.0 %copy-start.1 = (f32[3,4]{1,0:T(4,128)S(1)}, f32[3,4]{1,0:T(4,128)}, u32[]{:S(2)}) copy-start(f32[3,4]{1,0:T(4,128)} %get-tuple-element.10) | copy-start | bytes 148

commit v3 on v2

--- a/solution.py
+++ b/solution.py
@@ -291,12 +291,13 @@
 
     def reduce_ring(src, got, parts, k, pair):
         wait_recv(pair)
-        parts[z] = src[c] + got[...]
+        parts[z] = (src[c].astype(F32) + got[...].astype(F32)).astype(parts.dtype)
         return go([copy(parts.at[z], parts.at[z], k + d - 1, at_z(d)) for d in (1, 2, 3)])
 
     def reduce_back(parts, out, k, around):
         wait_recv(around)
-        out[c] = (parts[0] + parts[1]) + (parts[2] + parts[3])
+        four = [parts[n].astype(F32) for n in range(4)]
+        out[c] = ((four[0] + four[1]) + (four[2] + four[3])).astype(out.dtype)
         return go([copy(out.at[c], out.at[c], k, partner)])
 
     wait_recv(p_3)
@@ -337,31 +338,22 @@
         rlo[own_rows, :] = lo[y]
         return go([copy(lo.at[lax.rem(y + d, 4)], rlo.at[own_rows, :], k + d - 1, at_y(d)) for d in (1, 2, 3)])
 
-    wait_recv(g_3)
-
-    def factor(i, a):
-        wi[i] = inverse_factor(a)
-
-    def rest(i, j):
-        return g_out[(i * (i + 1) // 2 + j) // 3, (i * (i + 1) // 2 + j) % 3] / total
-
-    factor(0, rest(0, 0))
-
     def left_over(copies):
         return [got for got in copies if any(got is other for other in awaited)]
 
+    def part(ref, zz, *lead):
+        return ref.at[(*lead, pl.ds(pl.multiple_of(zz * group, group), group), slice(None))]
+
+    def cross_pair(v, src, got):
+        rows = v.shape[0] // 2
+        src[0] = v[:rows].astype(src.dtype)
+        src[1] = v[rows:].astype(src.dtype)
+        return reduce_pair(src, got, sems(1))
+
     for i in range(4):
         wait_recv(left_over(b_out[i] + b_on[i]))
-    hk = sems(1)
     other_half = pl.ds(pl.multiple_of((1 - c) * half, half), half)
     own_half = pl.ds(pl.multiple_of(c * half, half), half)
-    h_in[1] = nt(btg[other_half, :], pa[:p2, :])
-    h_1 = go([copy(h_in.at[1], h_r, hk, partner)])
-    h_in[0] = nt(btg[own_half, :], pa[:p2, :])
-
-    def part(ref, zz, *lead):
-        return ref.at[(*lead, pl.ds(pl.multiple_of(zz * group, group), group), slice(None))]
-
     ck, cz = sems(4), sems(12)
     c_1, c_2 = [], []
 
@@ -380,35 +372,46 @@
             go([copy(part(c_s, lax.rem(z + d, 4), j), c_z.at[j, d - 1], cz + 3 * j + d - 1, at_z(d)) for d in (1, 2, 3)])
         )
 
+    hk = sems(1)
+    h_in[1] = nt(btg[other_half, :], pa[:p2, :]).astype(BF16)
+    h_1 = go([copy(h_in.at[1], h_r, hk, partner)])
+    h_in[0] = nt(btg[own_half, :], pa[:p2, :]).astype(BF16)
     correlate(0)
     wait_recv(h_1)
-    h_s[...] = h_in[0] + h_r[...]
+    h_s[...] = (h_in[0].astype(F32) + h_r[...].astype(F32)).astype(BF16)
     k = sems(3)
     h_2 = go([copy(part(h_s, lax.rem(z + d, 4)), h_z.at[d - 1], k + d - 1, at_z(d)) for d in (1, 2, 3)])
+    for j in range(4):
+        wait_recv(left_over(r_out[j] + r_on[j]))
+    x_1 = cross_pair(nn(pa[:p2, :], rg[y]), x_in, x_r)
+    correlate(1)
     pass_on(0)
+    x_2 = reduce_ring(x_in, x_r, x_z, sems(3), x_1)
+    lows = lows_on()
+
+    wait_recv(g_3)
+
+    def factor(i, a):
+        wi[i] = inverse_factor(a)
+
+    def rest(i, j):
+        return g_out[(i * (i + 1) // 2 + j) // 3, (i * (i + 1) // 2 + j) % 3] / total
+
+    factor(0, rest(0, 0))
     w00 = wi[0]
     l10, l20 = nt(rest(1, 0), w00, HIGHEST), nt(rest(2, 0), w00, HIGHEST)
-    factor(1, rest(1, 1) - nt(l10, l10, HIGHEST))
-    correlate(1)
-    lows = lows_on()
     pass_on(1)
     correlate(2)
+    x_3 = reduce_back(x_z, x_out, sems(1), x_2)
+    factor(1, rest(1, 1) - nt(l10, l10, HIGHEST))
+    pass_on(2)
+    correlate(3)
     w11 = wi[1]
     l21 = nt(rest(2, 1) - nt(l20, l10, HIGHEST), w11, HIGHEST)
     factor(2, rest(2, 2) - nt(l20, l20, HIGHEST) - nt(l21, l21, HIGHEST))
-    pass_on(2)
-    for j in range(4):
-        wait_recv(left_over(r_out[j] + r_on[j]))
-
-    def cross_pair(v, src, got):
-        src[0] = v[: p3 // 2]
-        src[1] = v[p3 // 2 :]
-        return reduce_pair(src, got, sems(1))
-
-    x_1 = cross_pair(nn(pa[...], rg[y]), x_in, x_r)
-    correlate(3)
-    x_2 = reduce_ring(x_in, x_r, x_z, sems(3), x_1)
     pass_on(3)
+    wait_recv(lows)
+    v_1 = cross_pair(nn(pa[...], rg[y]) + nn(pa[...], rlo[...]), v_in, v_r)
     w22 = wi[2]
     w10 = -nn(w11, nn(l10, w00, HIGHEST), HIGHEST)
     w20 = -nn(w22, nn(l20, w00, HIGHEST) + nn(l21, w10, HIGHEST), HIGHEST)
@@ -422,29 +425,23 @@
         ],
         axis=0,
     )
-    x_3 = reduce_back(x_z, x_out, sems(1), x_2)
     eye3 = jnp.where(iota((p3, p3), 0) == iota((p3, p3), 1), 1.0, 0.0).astype(F32)
     wtm[...] = nt(eye3, wm[...], HIGHEST)
     wait_recv(x_3)
-    cross = jnp.concatenate([x_out[0], x_out[1]], axis=0) / total
-    coef = nn(wm[:p2, :p2], cross[:p2], HIGHEST)
+    cross = jnp.concatenate([x_out[0], x_out[1]], axis=0).astype(F32) / total
+    coef = nn(wm[:p2, :p2], cross, HIGHEST)
     cg[y] = coef.astype(BF16)
     k = sems(3)
     cg_1 = go([copy(cg.at[y], cg.at[y], k + d - 1, at_y(d)) for d in (1, 2, 3)])
-    wait_recv(lows)
-    v_1 = cross_pair(nn(pa[...], rlo[...]), v_in, v_r)
-    for q in range(2):
+    v_2 = reduce_ring(v_in, v_r, v_z, sems(3), v_1)
+    for q in range(4):
         at = slice(q * q4, (q + 1) * q4)
         residual[at, :] = nn(pit[at, :], rg[y]) + nn(pit[at, :], rlo[...])
-    v_2 = reduce_ring(v_in, v_r, v_z, sems(3), v_1)
-    for q in range(2, 4):
-        at = slice(q * q4, (q + 1) * q4)
-        residual[at, :] = nn(pit[at, :], rg[y]) + nn(pit[at, :], rlo[...])
 
     def settle():
         wait_recv(v_3)
-        low = jnp.concatenate([v_out[0], v_out[1]], axis=0) / total
-        coef = nn(wm[...], cross + low, HIGHEST)
+        full = jnp.concatenate([v_out[0], v_out[1]], axis=0) / total
+        coef = nn(wm[...], full, HIGHEST)
         coefs[...] = coef
         y_hi, y_lo = split(nn(wtm[...], coef, HIGHEST))
         for q in range(4):
@@ -452,7 +449,8 @@
             residual[at, :] = residual[at, :] - (tn(ptf[q], y_hi) + tn(ptf[q], y_lo))
 
     wait_recv(h_2)
-    h_all = part(h_s, z)[...] + h_z[0] + (h_z[1] + h_z[2])
+    four = [v.astype(F32) for v in (part(h_s, z)[...], h_z[0], h_z[1], h_z[2])]
+    h_all = (four[0] + four[1]) + (four[2] + four[3])
     hn = nt(h_all, wm[:p2, :p2], HIGHEST).astype(BF16)
     first = jnp.where(iota((group, p2), 1) < bl, hn.astype(F32), 0.0).astype(BF16)
     wait_recv(cg_1)
@@ -475,7 +473,6 @@
     v_3 = reduce_back(v_z, v_out, sems(1), v_2)
     k = sems(3)
     s_1 = go([copy(sx.at[x], sx.at[x], k + d - 1, at_x(d)) for d in (1, 2, 3)])
-    settle()
     wait_recv(s_1)
     sg[s] = (sx[0] + sx[1]) + (sx[2] + sx[3])
     ks = sems(1)
@@ -485,6 +482,7 @@
         return carry
 
     lax.fori_loop(1, 8, tell, 0)
+    settle()
     wait_recv(track([Bulk(sg.at[pl.ds(0, 7)], ss.at[ks], rs.at[ks])]))
     out = jnp.zeros((8, 128), F32)
     for i in range(2):
@@ -522,8 +520,9 @@
         ((nr, nr), BF16), ((4 * tslab, nr), BF16),
         ((4, nr, slab), BF16), ((4, q4, slab), BF16), ((nr, slab), BF16), ((p3, nr), BF16),
         ((2, 3, bl, bl), F32), ((3, bl, bl), F32), ((4, 3, bl, bl), F32), ((2, 3, bl, bl), F32),
-        *[((2, p3 // 2, slab), F32), ((p3 // 2, slab), F32), ((4, p3 // 2, slab), F32), ((2, p3 // 2, slab), F32)] * 2,
-        ((2, half, p2), F32), ((half, p2), F32), ((half, p2), F32), ((3, group, p2), F32),
+        ((2, bl, slab), BF16), ((bl, slab), BF16), ((4, bl, slab), BF16), ((2, bl, slab), BF16),
+        ((2, p3 // 2, slab), F32), ((p3 // 2, slab), F32), ((4, p3 // 2, slab), F32), ((2, p3 // 2, slab), F32),
+        ((2, half, p2), BF16), ((half, p2), BF16), ((half, p2), BF16), ((3, group, p2), BF16),
         ((4, half, slab), F32), ((4, half, slab), BF16), ((4, half, slab), BF16), ((4, half, slab), BF16),
         ((4, 3, group, slab), BF16), ((4, p2, slab), BF16), ((4, 8, 128), F32), ((8, 8, 128), F32),
         ((3, bl, bl), F32), ((p3, p3), F32), ((p3, p3), F32),

time: 95.2 us -> 90.8 us (0.954)
  Pallas kernels: 87.1 us -> 82.7 us
    pallas_call x1, Pallas kernels: 87.1 us -> 82.7 us  [local(): pl.pallas_call(functools.partial(body, dims), out_shape=(jax.ShapeDtypeSt...]
where the time goes in v3:
time: 90.8 us; the launch traced here: 90.5 us
  Pallas kernels  82.7 us (91%)
  local copies, waits for them, and re-layouts  5.38 us (6%)
  other arithmetic  1.73 us (2%)
    pallas_call x1, Pallas kernels, local(): pl.pallas_call(functools.partial(body, dims), out_shape=(jax.ShapeDtypeSt...  82.7 us
    unnamed x7, local copies, waits for them, and re-layouts  3.56 us

profile of v3, /device:TPU:1, one launch (start us, length us, event | category | flops | bytes accessed | tf_op | source)
XLA Modules:
  0.0 90.5 jit_solution(16453210862825370210)
XLA Ops:
  0.6 0.1 iota_compare_fusion.1
  0.7 0.8 reshape.105
  1.6 0.1 broadcast_compare_fusion
  1.6 0.1 copy.14
  1.7 0.8 convert_reduce_fusion
  2.5 0.1 copy.16
  2.6 0.1 select_reduce_fusion
  2.7 0.2 convert_reduce_fusion.1
  2.9 0.5 bitcast_add_fusion.place
  3.4 0.1 copy.17
  3.5 0.7 reshape.107.index
  4.2 82.7 %shard_map.67 = (f32[1024,256]{1,0:T(8,128)}, f32[192,256]{1,0:T(8,128)}, f32[3,4]{1,0:T(4,128)}) custom-call(s32[3]{0:T(128)} %chosen.1, s32[1,1024]{1,0:T(1,128)} %reshape.107.index, s32[1,64]{1,0:T(1,128)} %bitcast_add_fusion.place, bf16[1024,256]{1,0:T(8,128)(2,1)} %basis.1, f32[64,4096]{1,0:T(8,128)} %strain.1), custom_call_target="tpu_custom_call" | custom-call | tf_op jit(solution)/shard_map/pallas_call | solution.py:530
  86.9 0.0 copy-start
  87.0 0.0 copy-start.1
  87.0 2.3 %copy.23 = f32[1024,256]{1,0:T(8,128)} copy(f32[1024,256]{1,0:T(8,128)} %get-tuple-element.8) | data formatting | bytes 2097152
  89.3 0.0 copy-done
  89.3 0.7 copy.24
  89.9 0.0 copy-done.1
  89.9 0.6 copy.25
  (4 shorter events, 0.1 us)
Async XLA Ops:
  86.9 2.3 %copy-start = (f32[192,256]{1,0:T(8,128)S(1)}, f32[192,256]{1,0:T(8,128)}, u32[]{:S(2)}) copy-start(f32[192,256]{1,0:T(8,128)} %get-tuple-element.9) | copy-start | bytes 589828
  87.0 3.0 %copy-start.1 = (f32[3,4]{1,0:T(4,128)S(1)}, f32[3,4]{1,0:T(4,128)}, u32[]{:S(2)}) copy-start(f32[3,4]{1,0:T(4,128)} %get-tuple-element.10) | copy-start | bytes 148

commit v4 on v3

--- a/solution.py
+++ b/solution.py
@@ -83,10 +83,10 @@
 
 
 def body(
-    dims, chosen, index, place, basis, strain, residual, coefs, scores,
+    dims, chosen, route, basis, strain, residual, coefs, scores,
     ptp, prs, psum, pry, ptf, out_h, mid_h, in_h, out_l, mid_l, in_l, pit, btg, rg, lo, rlo, pa,
     g_in, g_r, g_z, g_out, x_in, x_r, x_z, x_out, v_in, v_r, v_z, v_out, h_in, h_r, h_s, h_z,
-    c_own, c_send, c_r, c_s, c_z, cg, sx, sg, wi, wm, wtm, ss, rs,
+    c_own, c_send, c_r, c_s, c_z, cg, sx, sg, wi, wm, wtm, index, ss, rs,
 ):
     rk, slab, tslab, bl = dims
     nr, q4, sr = 128 * rk, 32 * rk, 8 * rk
@@ -166,7 +166,17 @@
     for q in range(4):
         ptp[q] = nt(select, basis[q * q4 : (q + 1) * q4, :]).astype(BF16)
 
-    order = ones_where(iota((sr, sr), 0) == place[...])
+    bits, fold = nr.bit_length() - 1, 5
+    ahead = ones_where(
+        (iota((2 * sr, 2 * sr), 0) < iota((2 * sr, 2 * sr), 1))
+        & ((iota((2 * sr, 2 * sr), 0) >= sr) == (iota((2 * sr, 2 * sr), 1) >= sr))
+    )
+    own = route[pl.ds(s * 8 + t // 2, 1), :]
+    own = jnp.where(lax.rem(t, 2) == 1, own[:, sr:], own[:, :sr]) >> bits
+    to = iota((8, sr), 0) == own
+    place = nn(ones_where(to), ahead[:sr, :sr]) + (iota((8, sr), 0) * rk).astype(F32)
+    place = jnp.sum(jnp.where(to, place, 0.0), axis=0, keepdims=True)
+    order = ones_where(iota((sr, sr), 0).astype(F32) == place)
 
     def packed(v):
         pair = [v[:, n * wide : (n + 1) * wide].reshape(8, rk, wide) for n in (0, 1)]
@@ -185,6 +195,23 @@
         return carry
 
     lax.fori_loop(0, 4, sort_slab, 0)
+
+    hit = (route[...] >> bits) == s
+    code = jnp.where(hit, nn(ones_where(hit), ahead) + 1.0, 0.0).astype(BF16)
+    spot = route[...] & (nr - 1)
+    high, low = (spot >> fold).astype(F32).astype(BF16), (spot & ((1 << fold) - 1)).astype(F32).astype(BF16)
+    at = iota((q4, 64), 0)
+    px, ps = at // sr, lax.rem(at // rk, 8)
+    back = iota((q4, 2 * sr), 0)
+    half_of = lax.rem(back // sr, 2) == (iota((q4, 2 * sr), 1) >= sr).astype(jnp.int32)
+    turn = (lax.rem(back, rk) + 1).astype(F32)
+    every = jnp.ones((8, 2 * sr), BF16)
+    for q in range(4):
+        pick = ones_where(iota((q4, 64), 1) == ps * 8 + q * 2 + px // 2)
+        here = half_of & (nn(pick, code) == turn)
+        big = nt(every, jnp.where(here, nn(pick, high), 0.0).astype(BF16))
+        small = nt(every, jnp.where(here, nn(pick, low), 0.0).astype(BF16))
+        index[:, q * q4 : (q + 1) * q4] = (big[:1] * (1 << fold) + small[:1]).astype(jnp.int32)
 
     pl.semaphore_wait(barrier, 13)
 
@@ -499,20 +526,6 @@
     nr, q4, sr = 128 * rk, 32 * rk, 8 * rk
     p3, p2 = 3 * bl, 2 * bl
     half, group = 2 * tslab, tslab // 2
-    s, t = lax.axis_index("samp"), lax.axis_index("term")
-
-    routes = route.reshape(128, sr)
-    goes = routes // nr
-    hit = goes == s
-    before = jnp.tril(jnp.ones((sr, sr), jnp.bool_), -1)
-    rank = jnp.sum(jnp.where(before[None], hit[:, None, :], False), axis=2)
-    slot = hit[:, :, None] & (rank[:, :, None] == jnp.arange(rk)[None, None, :])
-    sample = jnp.sum(jnp.where(slot, (routes - goes * nr)[:, :, None], 0), axis=1)
-    index = sample.reshape(8, 4, 4, rk).transpose(1, 2, 0, 3).reshape(1, nr)
-    own = lax.dynamic_index_in_dim(goes, s * 16 + t, 0, keepdims=False)
-    same = (own[:, None] == own[None, :]) & before
-    place = (own * rk + jnp.sum(same, axis=1)).reshape(1, sr)
-
     vmem = pl.BlockSpec(memory_space=pltpu.VMEM)
     scratch = [
         ((4, p3, q4), BF16), ((3, p3, q4), BF16), ((p3, q4), BF16), ((3, p3, q4), BF16), ((4, p3, q4), BF16),
@@ -525,7 +538,7 @@
         ((2, half, p2), BF16), ((half, p2), BF16), ((half, p2), BF16), ((3, group, p2), BF16),
         ((4, half, slab), F32), ((4, half, slab), BF16), ((4, half, slab), BF16), ((4, half, slab), BF16),
         ((4, 3, group, slab), BF16), ((4, p2, slab), BF16), ((4, 8, 128), F32), ((8, 8, 128), F32),
-        ((3, bl, bl), F32), ((p3, p3), F32), ((p3, p3), F32),
+        ((3, bl, bl), F32), ((p3, p3), F32), ((p3, p3), F32), ((1, nr), jnp.int32),
     ]
     return pl.pallas_call(
         functools.partial(body, dims),
@@ -534,14 +547,14 @@
             jax.ShapeDtypeStruct((p3, slab), F32),
             jax.ShapeDtypeStruct((3, tslab // bl), F32),
         ),
-        in_specs=[pl.BlockSpec(memory_space=pltpu.SMEM), vmem, vmem, vmem, vmem],
+        in_specs=[pl.BlockSpec(memory_space=pltpu.SMEM), vmem, vmem, vmem],
         out_specs=(vmem, vmem, vmem),
         scratch_shapes=[pltpu.VMEM(shape, dtype) for shape, dtype in scratch]
         + [pltpu.SemaphoreType.DMA((128,)), pltpu.SemaphoreType.DMA((128,))],
         compiler_params=pltpu.CompilerParams(
             collective_id=0, has_side_effects=True, vmem_limit_bytes=60 * 1024 * 1024
         ),
-    )(chosen, index, place, basis, strain)
+    )(chosen, route.reshape(64, 2 * sr), basis, strain)
 
 
 def solution(mesh, dims=(8, 256, 256, BLOCK)):

time: 90.8 us -> 88.7 us (0.977)
  local copies, waits for them, and re-layouts: 5.38 us -> 3.57 us
  other arithmetic: 1.73 us -> 0 us
  Pallas kernels: 82.7 us -> 84.3 us
    pallas_call x1, Pallas kernels: 82.7 us -> 84.3 us  [local(): pl.pallas_call(functools.partial(body, dims), out_shape=(jax.ShapeDtypeSt...]
    reshape x2 -> x0, local copies, waits for them, and re-layouts: 1.53 us -> none  [the longest x1 0.84 us: local(): routes = route.reshape(128, sr)]
    reduce_sum x3 -> x0, other arithmetic: 1.02 us -> none  [the longest x1 0.75 us: local(): rank = jnp.sum(jnp.where(before[None], hit[:, None, :], False), axis=2)]
where the time goes in v4:
time: 88.7 us; the launch traced here: 88.5 us
  Pallas kernels  84.3 us (95%)
  local copies, waits for them, and re-layouts  3.57 us (4%)
    pallas_call x1, Pallas kernels, local(): pl.pallas_call(functools.partial(body, dims), out_shape=(jax.ShapeDtypeSt...  84.3 us
    unnamed x7, local copies, waits for them, and re-layouts  3.57 us

profile of v4, /device:TPU:1, one launch (start us, length us, event | category | flops | bytes accessed | tf_op | source)
XLA Modules:
  0.0 88.5 jit_solution(4763989705498591718)
XLA Ops:
  0.6 84.3 %shard_map.67 = (f32[1024,256]{1,0:T(8,128)}, f32[192,256]{1,0:T(8,128)}, f32[3,4]{1,0:T(4,128)}) custom-call(s32[3]{0:T(128)} %chosen.1, s32[64,128]{1,0:T(8,128)} %bitcast.1, bf16[1024,256]{1,0:T(8,128)(2,1)} %basis.1, f32[64,4096]{1,0:T(8,128)} %strain.1), custom_call_target="tpu_custom_call" | custom-call | tf_op jit(solution)/shard_map/pallas_call | solution.py:543
  84.9 0.0 copy-start
  84.9 2.3 %copy.10 = f32[1024,256]{1,0:T(8,128)} copy(f32[1024,256]{1,0:T(8,128)} %get-tuple-element.6) | data formatting | bytes 2097152
  87.2 0.0 copy-done
  87.2 0.0 copy-start.1
  87.2 0.7 copy.11
  87.9 0.0 copy-done.1
  87.9 0.6 copy.12
Async XLA Ops:
  84.9 2.3 %copy-start = (f32[192,256]{1,0:T(8,128)S(1)}, f32[192,256]{1,0:T(8,128)}, u32[]{:S(2)}) copy-start(f32[192,256]{1,0:T(8,128)} %get-tuple-element.7) | copy-start | bytes 589828
  87.2 0.7 copy-start.1

commit v5 on v4

--- a/solution.py
+++ b/solution.py
@@ -408,11 +408,11 @@
     h_s[...] = (h_in[0].astype(F32) + h_r[...].astype(F32)).astype(BF16)
     k = sems(3)
     h_2 = go([copy(part(h_s, lax.rem(z + d, 4)), h_z.at[d - 1], k + d - 1, at_z(d)) for d in (1, 2, 3)])
+    correlate(1)
+    pass_on(0)
     for j in range(4):
         wait_recv(left_over(r_out[j] + r_on[j]))
     x_1 = cross_pair(nn(pa[:p2, :], rg[y]), x_in, x_r)
-    correlate(1)
-    pass_on(0)
     x_2 = reduce_ring(x_in, x_r, x_z, sems(3), x_1)
     lows = lows_on()
 

time: 88.7 us -> 87.9 us (level)
  no operation moved by 1% of the time
where the time goes in v5:
time: 87.9 us; the launch traced here: 87.7 us
  Pallas kernels  83.5 us (95%)
  local copies, waits for them, and re-layouts  3.57 us (4%)
    pallas_call x1, Pallas kernels, local(): pl.pallas_call(functools.partial(body, dims), out_shape=(jax.ShapeDtypeSt...  83.5 us
    unnamed x7, local copies, waits for them, and re-layouts  3.57 us

profile of v5, /device:TPU:1, one launch (start us, length us, event | category | flops | bytes accessed | tf_op | source)
XLA Modules:
  0.0 87.7 jit_solution(18328008272406195064)
XLA Ops:
  0.6 83.5 %shard_map.67 = (f32[1024,256]{1,0:T(8,128)}, f32[192,256]{1,0:T(8,128)}, f32[3,4]{1,0:T(4,128)}) custom-call(s32[3]{0:T(128)} %chosen.1, s32[64,128]{1,0:T(8,128)} %bitcast.1, bf16[1024,256]{1,0:T(8,128)(2,1)} %basis.1, f32[64,4096]{1,0:T(8,128)} %strain.1), custom_call_target="tpu_custom_call" | custom-call | tf_op jit(solution)/shard_map/pallas_call | solution.py:543
  84.2 0.0 copy-start
  84.2 2.3 %copy.10 = f32[1024,256]{1,0:T(8,128)} copy(f32[1024,256]{1,0:T(8,128)} %get-tuple-element.6) | data formatting | bytes 2097152
  86.5 0.0 copy-done
  86.5 0.0 copy-start.1
  86.5 0.7 copy.11
  87.2 0.0 copy-done.1
  87.2 0.6 copy.12
Async XLA Ops:
  84.2 2.3 %copy-start = (f32[192,256]{1,0:T(8,128)S(1)}, f32[192,256]{1,0:T(8,128)}, u32[]{:S(2)}) copy-start(f32[192,256]{1,0:T(8,128)} %get-tuple-element.7) | copy-start | bytes 589828
  86.5 0.7 copy-start.1
